TPU v7x, 256 devices: a whole 4x4x8 slice. The times are simulated.
256 devices in a mesh: gx: 64 (over z, x, core), gy: 4 (over y).
Axes of the slice: x: 4, y: 4, z: 8, core: 2. Of those that a mesh axis runs over, the one named last changes fastest.
Arguments:
- positions: float32 [3, 262144], P(None, 'gx'), may hold values from -6 to 6
- strengths: float32 [3, 262144], P(None, 'gx'), may hold values from -4 to 4
- core_radii: float32 [262144], P('gx'), may hold values from 0.1 to 0.4
- tile_pairs: int32 [2048, 2], replicated, may hold values from 0 to 255, as said below
- block_home: int32 [256], replicated, may hold values from 0 to 255, as said below
Outputs:
- velocity: float32 [3, 262144], P(None, 'gx')
- stretching: float32 [3, 262144], P(None, 'gx')
Inputs may be any that keep to these rules, and one draw needn't show every extreme that they name: `tile_pairs`: each row names two different logical blocks, the smaller first. The 8 rows of one device name 16 distinct logical blocks, and at most 1 of them are stored on one gx index (storage block s is held by gx index s // 4); some gx index holds 1 of them for every device. `block_home`: A permutation of the blocks. The particles stay sharded because they are the wake solver's distributed state, and the listed pairs are the near-field part of a tree-code evaluation.
All inputs are finite; a program needn't handle non-finite values.
Results may differ from a plain program's by a relative error of at most 0.0003.
Values sent between devices are 32-bit elements; how exact they have to be, the bound alone decides.
A program may use at most 64 MiB of HBM per device.

v0:
```python
import jax
import jax.numpy as jnp
from jax import lax
from jax.sharding import PartitionSpec as P

BS = 1024
TILES_DEV = 8


inv_four_pi = 0.07957747154594767


def cross_product(a, b):
    return (a[1] * b[2] - a[2] * b[1], a[2] * b[0] - a[0] * b[2], a[0] * b[1] - a[1] * b[0])


def tile_rates(first, second):
    x_first = [first[k][:, None] for k in range(3)]
    w_first = [first[3 + k][:, None] for k in range(3)]
    sigma_first = first[6][:, None]
    x_second = [second[k][None, :] for k in range(3)]
    w_second = [second[3 + k][None, :] for k in range(3)]
    sigma_second = second[6][None, :]
    r = [x_first[k] - x_second[k] for k in range(3)]
    g = (
        r[0] * r[0]
        + r[1] * r[1]
        + r[2] * r[2]
        + 0.5 * (sigma_first * sigma_first + sigma_second * sigma_second)
    )
    q = lax.rsqrt(g)
    f = -inv_four_pi * q * q * q
    h = -3.0 * f * q * q
    turn_second = cross_product(r, w_second)
    turn_first = cross_product(r, w_first)
    spin = cross_product(w_first, w_second)
    along_first = r[0] * w_first[0] + r[1] * w_first[1] + r[2] * w_first[2]
    along_second = r[0] * w_second[0] + r[1] * w_second[1] + r[2] * w_second[2]
    rates_first = [jnp.sum(f * turn_second[k], axis=1) for k in range(3)]
    rates_first = rates_first + [
        jnp.sum(f * spin[k] + h * along_first * turn_second[k], axis=1) for k in range(3)
    ]
    rates_second = [-jnp.sum(f * turn_first[k], axis=0) for k in range(3)]
    rates_second = rates_second + [
        jnp.sum(h * along_second * turn_first[k] - f * spin[k], axis=0) for k in range(3)
    ]
    return (jnp.stack(rates_first), jnp.stack(rates_second))


def split_rates(first, second):
    piece = min(512, first.shape[1])
    gained_rows = []
    gained_other = jnp.zeros((6, second.shape[1]), jnp.float32)
    for start in range(0, first.shape[1], piece):
        part_rows, part_other = tile_rates(first[:, start : start + piece], second)
        gained_rows.append(part_rows)
        gained_other = gained_other + part_other
    return (jnp.concatenate(gained_rows, 1), gained_other)


def storage_of(logical, block_home):
    identity = jnp.arange(block_home.shape[0], dtype=jnp.int32)
    match = logical[..., None] == identity
    return jnp.sum(jnp.where(match, block_home, 0), axis=-1)


def body(positions, strengths, core_radii, tile_pairs, block_home):
    gx_count = lax.axis_size("gx")
    gy_count = lax.axis_size("gy")
    my_column = lax.axis_index("gx")
    my_row = lax.axis_index("gy")
    resident = jnp.concatenate([positions, strengths, core_radii[None, :]], 0)
    requests = 2 * TILES_DEV
    grouped = tile_pairs.reshape(gx_count, gy_count, requests)
    row_pairs = lax.dynamic_index_in_dim(grouped, my_row, 1, keepdims=False)
    stored = storage_of(row_pairs, block_home)
    my_stored = lax.dynamic_index_in_dim(stored, my_column, 0, keepdims=False)
    everything = lax.all_gather(resident, "gx", axis=1, tiled=True).reshape(7, -1, BS)
    blocks = jnp.take(everything, my_stored, axis=1)
    tile_blocks = jnp.moveaxis(blocks.reshape(7, TILES_DEV, 2, BS), 1, 0)

    def one_tile(carry, tile):
        gained_first, gained_second = split_rates(tile[:, 0], tile[:, 1])
        return (carry, jnp.stack([gained_first, gained_second], 1))

    partials = lax.scan(one_tile, jnp.int32(0), tile_blocks)[1]
    partials = jnp.moveaxis(partials, 0, 1).reshape(6, requests, BS)
    totals = jnp.zeros((6, block_home.shape[0], BS), jnp.float32).at[:, my_stored].add(partials)
    share = lax.psum_scatter(totals.reshape(6, -1), "gx", scatter_dimension=1, tiled=True)
    rates = lax.psum(share, "gy")
    return (rates[:3], rates[3:])


def solution(mesh):
    return jax.shard_map(
        body,
        mesh=mesh,
        in_specs=(P(None, "gx"), P(None, "gx"), P("gx"), P(), P()),
        out_specs=(P(None, "gx"), P(None, "gx")),
        check_vma=False,
    )
```

profile of v0, /device:TPU:1, one launch (start us, length us, event | category | flops | bytes accessed | tf_op | source)
XLA Modules:
  0.0 443.4 jit_solution(5528078988186684600)
XLA Ops:
  7.2 0.0 copy-start
  7.2 0.0 all-gather.2.cloned.1.call-start
  7.2 1.6 pad_maximum_fusion.1
  8.8 0.0 all-gather.2.cloned.1.call-update
  8.8 0.0 reduce-scatter.2.cloned.1.call-start
  8.9 1.1 copy.17
  10.0 0.3 reshape.324
  10.4 0.0 copy-done
  10.4 1.3 select_reduce_fusion
  11.7 0.1 squeeze.15
  11.8 86.2 %all-gather.2.cloned.1.call-done = f32[7,262144]{1,0:T(8,128)} async-done(((f32[7,4096]{1,0:T(8,128)}), f32[7,262144]{1,0:T(8,128)}) %all-gather.2.cloned.1.call-update) | async-done | bytes 7340048 | tf_op jit(solution)/shard_map/all_gather | solution.py:78
  98.0 4.0 gather_fusion
  102.0 0.5 fusion.93
  102.5 131.6 %while.10 = (s32[]{:T(128)}, f32[8,6,2,1024]{3,2,1,0:T(2,128)S(1)}, f32[8,7,2,1024]{3,2,0,1:T(2,128)S(1)}, s32[]{:T(128)}) while((s32[]{:T(128)}, f32[8,6,2,1024]{3,2,1,0:T(2,128)S(1)}, f32[8,7,2,1024]{3,2,0,1:T(2,128)S(1)}, s32[]{:T(128)}) %tuple.78), condition=%wide.region_26.27_spmd, body=%wide.region_1.26_spmd.sunk | while | flops 93337600 | bytes 970821 | solution.py:86
  102.6 7.9 %fusion.106 = (f32[1024]{0:T(1024)S(1)}, f32[1024]{0:T(1024)S(1)}, f32[1024]{0:T(1024)S(1)}, f32[512]{0:T(512)S(1)}, f32[512]{0:T(512)S(1)}, /*index=5*/f32[512]...) fusion(f32[512]{0:T(512)S(1)} %bitcast.218, ...), kind=kLoop, calls=%fused_computation.73.clone.1 | loop fusion | flops 46652416 | bytes 79872 | tf_op jit(solution)/shard_map/while/body/eval_jaxpr/reduce_sum | solution.py:45
  110.5 7.9 %fusion.107 = (f32[1024]{0:T(1024)S(1)}, f32[1024]{0:T(1024)S(1)}, f32[1024]{0:T(1024)S(1)}, f32[512]{0:T(512)S(1)}, f32[512]{0:T(512)S(1)}, /*index=5*/f32[512]...) fusion(f32[512]{0:T(512)S(1)} %bitcast.212, ...), kind=kLoop, calls=%fused_computation.119.clone.1 | loop fusion | flops 46652416 | bytes 79872 | tf_op jit(solution)/shard_map/while/body/eval_jaxpr/reduce_sum | solution.py:45
  118.8 0.1 fusion.108
  119.1 7.9 %fusion.106 = (f32[1024]{0:T(1024)S(1)}, f32[1024]{0:T(1024)S(1)}, f32[1024]{0:T(1024)S(1)}, f32[512]{0:T(512)S(1)}, f32[512]{0:T(512)S(1)}, /*index=5*/f32[512]...) fusion(f32[512]{0:T(512)S(1)} %bitcast.218, ...), kind=kLoop, calls=%fused_computation.73.clone.1 | loop fusion | flops 46652416 | bytes 79872 | tf_op jit(solution)/shard_map/while/body/eval_jaxpr/reduce_sum | solution.py:45
  127.0 7.9 %fusion.107 = (f32[1024]{0:T(1024)S(1)}, f32[1024]{0:T(1024)S(1)}, f32[1024]{0:T(1024)S(1)}, f32[512]{0:T(512)S(1)}, f32[512]{0:T(512)S(1)}, /*index=5*/f32[512]...) fusion(f32[512]{0:T(512)S(1)} %bitcast.212, ...), kind=kLoop, calls=%fused_computation.119.clone.1 | loop fusion | flops 46652416 | bytes 79872 | tf_op jit(solution)/shard_map/while/body/eval_jaxpr/reduce_sum | solution.py:45
  135.3 0.1 fusion.108
  135.5 7.9 %fusion.106 = (f32[1024]{0:T(1024)S(1)}, f32[1024]{0:T(1024)S(1)}, f32[1024]{0:T(1024)S(1)}, f32[512]{0:T(512)S(1)}, f32[512]{0:T(512)S(1)}, /*index=5*/f32[512]...) fusion(f32[512]{0:T(512)S(1)} %bitcast.218, ...), kind=kLoop, calls=%fused_computation.73.clone.1 | loop fusion | flops 46652416 | bytes 79872 | tf_op jit(solution)/shard_map/while/body/eval_jaxpr/reduce_sum | solution.py:45
  143.5 7.9 %fusion.107 = (f32[1024]{0:T(1024)S(1)}, f32[1024]{0:T(1024)S(1)}, f32[1024]{0:T(1024)S(1)}, f32[512]{0:T(512)S(1)}, f32[512]{0:T(512)S(1)}, /*index=5*/f32[512]...) fusion(f32[512]{0:T(512)S(1)} %bitcast.212, ...), kind=kLoop, calls=%fused_computation.119.clone.1 | loop fusion | flops 46652416 | bytes 79872 | tf_op jit(solution)/shard_map/while/body/eval_jaxpr/reduce_sum | solution.py:45
  151.7 0.1 fusion.108
  152.0 7.9 %fusion.106 = (f32[1024]{0:T(1024)S(1)}, f32[1024]{0:T(1024)S(1)}, f32[1024]{0:T(1024)S(1)}, f32[512]{0:T(512)S(1)}, f32[512]{0:T(512)S(1)}, /*index=5*/f32[512]...) fusion(f32[512]{0:T(512)S(1)} %bitcast.218, ...), kind=kLoop, calls=%fused_computation.73.clone.1 | loop fusion | flops 46652416 | bytes 79872 | tf_op jit(solution)/shard_map/while/body/eval_jaxpr/reduce_sum | solution.py:45
  159.9 7.9 %fusion.107 = (f32[1024]{0:T(1024)S(1)}, f32[1024]{0:T(1024)S(1)}, f32[1024]{0:T(1024)S(1)}, f32[512]{0:T(512)S(1)}, f32[512]{0:T(512)S(1)}, /*index=5*/f32[512]...) fusion(f32[512]{0:T(512)S(1)} %bitcast.212, ...), kind=kLoop, calls=%fused_computation.119.clone.1 | loop fusion | flops 46652416 | bytes 79872 | tf_op jit(solution)/shard_map/while/body/eval_jaxpr/reduce_sum | solution.py:45
  168.2 0.1 fusion.108
  168.4 7.9 %fusion.106 = (f32[1024]{0:T(1024)S(1)}, f32[1024]{0:T(1024)S(1)}, f32[1024]{0:T(1024)S(1)}, f32[512]{0:T(512)S(1)}, f32[512]{0:T(512)S(1)}, /*index=5*/f32[512]...) fusion(f32[512]{0:T(512)S(1)} %bitcast.218, ...), kind=kLoop, calls=%fused_computation.73.clone.1 | loop fusion | flops 46652416 | bytes 79872 | tf_op jit(solution)/shard_map/while/body/eval_jaxpr/reduce_sum | solution.py:45
  176.4 7.9 %fusion.107 = (f32[1024]{0:T(1024)S(1)}, f32[1024]{0:T(1024)S(1)}, f32[1024]{0:T(1024)S(1)}, f32[512]{0:T(512)S(1)}, f32[512]{0:T(512)S(1)}, /*index=5*/f32[512]...) fusion(f32[512]{0:T(512)S(1)} %bitcast.212, ...), kind=kLoop, calls=%fused_computation.119.clone.1 | loop fusion | flops 46652416 | bytes 79872 | tf_op jit(solution)/shard_map/while/body/eval_jaxpr/reduce_sum | solution.py:45
  184.6 0.1 fusion.108
  184.9 7.9 %fusion.106 = (f32[1024]{0:T(1024)S(1)}, f32[1024]{0:T(1024)S(1)}, f32[1024]{0:T(1024)S(1)}, f32[512]{0:T(512)S(1)}, f32[512]{0:T(512)S(1)}, /*index=5*/f32[512]...) fusion(f32[512]{0:T(512)S(1)} %bitcast.218, ...), kind=kLoop, calls=%fused_computation.73.clone.1 | loop fusion | flops 46652416 | bytes 79872 | tf_op jit(solution)/shard_map/while/body/eval_jaxpr/reduce_sum | solution.py:45
  192.8 7.9 %fusion.107 = (f32[1024]{0:T(1024)S(1)}, f32[1024]{0:T(1024)S(1)}, f32[1024]{0:T(1024)S(1)}, f32[512]{0:T(512)S(1)}, f32[512]{0:T(512)S(1)}, /*index=5*/f32[512]...) fusion(f32[512]{0:T(512)S(1)} %bitcast.212, ...), kind=kLoop, calls=%fused_computation.119.clone.1 | loop fusion | flops 46652416 | bytes 79872 | tf_op jit(solution)/shard_map/while/body/eval_jaxpr/reduce_sum | solution.py:45
  201.1 0.1 fusion.108
  201.3 7.9 %fusion.106 = (f32[1024]{0:T(1024)S(1)}, f32[1024]{0:T(1024)S(1)}, f32[1024]{0:T(1024)S(1)}, f32[512]{0:T(512)S(1)}, f32[512]{0:T(512)S(1)}, /*index=5*/f32[512]...) fusion(f32[512]{0:T(512)S(1)} %bitcast.218, ...), kind=kLoop, calls=%fused_computation.73.clone.1 | loop fusion | flops 46652416 | bytes 79872 | tf_op jit(solution)/shard_map/while/body/eval_jaxpr/reduce_sum | solution.py:45
  209.3 7.9 %fusion.107 = (f32[1024]{0:T(1024)S(1)}, f32[1024]{0:T(1024)S(1)}, f32[1024]{0:T(1024)S(1)}, f32[512]{0:T(512)S(1)}, f32[512]{0:T(512)S(1)}, /*index=5*/f32[512]...) fusion(f32[512]{0:T(512)S(1)} %bitcast.212, ...), kind=kLoop, calls=%fused_computation.119.clone.1 | loop fusion | flops 46652416 | bytes 79872 | tf_op jit(solution)/shard_map/while/body/eval_jaxpr/reduce_sum | solution.py:45
  217.6 0.1 fusion.108
  217.8 7.9 %fusion.106 = (f32[1024]{0:T(1024)S(1)}, f32[1024]{0:T(1024)S(1)}, f32[1024]{0:T(1024)S(1)}, f32[512]{0:T(512)S(1)}, f32[512]{0:T(512)S(1)}, /*index=5*/f32[512]...) fusion(f32[512]{0:T(512)S(1)} %bitcast.218, ...), kind=kLoop, calls=%fused_computation.73.clone.1 | loop fusion | flops 46652416 | bytes 79872 | tf_op jit(solution)/shard_map/while/body/eval_jaxpr/reduce_sum | solution.py:45
  225.7 7.9 %fusion.107 = (f32[1024]{0:T(1024)S(1)}, f32[1024]{0:T(1024)S(1)}, f32[1024]{0:T(1024)S(1)}, f32[512]{0:T(512)S(1)}, f32[512]{0:T(512)S(1)}, /*index=5*/f32[512]...) fusion(f32[512]{0:T(512)S(1)} %bitcast.212, ...), kind=kLoop, calls=%fused_computation.119.clone.1 | loop fusion | flops 46652416 | bytes 79872 | tf_op jit(solution)/shard_map/while/body/eval_jaxpr/reduce_sum | solution.py:45
  234.0 0.1 fusion.108
  234.1 0.3 reshape.337
  234.4 0.2 copy.21
  234.6 4.3 broadcast_in_dim.34
  238.9 2.7 scatter_fusion
  241.6 0.0 reduce-scatter.2.cloned.1.call-update
  241.6 0.0 all-reduce.2.cloned.1.call-start
  241.7 143.8 %reduce-scatter.2.cloned.1.call-done = f32[6,4096]{1,0:T(8,128)} async-done(((f32[6,262144]{1,0:T(8,128)}), f32[6,4096]{1,0:T(8,128)}) %reduce-scatter.2.cloned.1.call-update) | async-done | bytes 98320 | tf_op jit(solution)/shard_map/reduce_scatter | solution.py:89
  385.5 0.0 all-reduce.2.cloned.1.call-update
  385.5 49.7 %all-reduce.2.cloned.1.call-done = f32[6,4096]{1,0:T(8,128)} async-done(((f32[6,4096]{1,0:T(8,128)}), f32[6,4096]{1,0:T(8,128)}) %all-reduce.2.cloned.1.call-update) | async-done | bytes 98320 | tf_op jit(solution)/shard_map/psum | solution.py:90
  435.2 1.7 fusion.98
  (223 shorter events, 2.7 us)
Async XLA Ops:
  7.2 3.2 copy-start
  7.2 90.8 %all-gather.2.cloned.1.call-start = ((), (), s32[]{:S(2)}) async-start(), calls=%async_computation.1 | async-start | bytes 8519680 | tf_op jit(solution)/shard_map/all_gather | solution.py:78
  8.8 376.6 %reduce-scatter.2.cloned.1.call-start = ((), (), s32[]{:S(2)}) async-start(), calls=%async_computation.2 | async-start | bytes 8519680 | tf_op jit(solution)/shard_map/reduce_scatter | solution.py:89
  241.6 193.5 %all-reduce.2.cloned.1.call-start = ((), (), s32[]{:S(2)}) async-start(), calls=%async_computation.3 | async-start | bytes 262144 | tf_op jit(solution)/shard_map/psum | solution.py:90
Sparse Core Ops, SparseCore 0:
  10.8 87.1 all-gather.1
  241.8 143.6 reduce-scatter.1
  387.9 47.2 all-reduce.1
where the time goes:
time: 445 us; the launch traced here: 443 us
  waiting for transfers between devices  280 us (63%)
  other arithmetic  134 us (30%)
  between operations  13.9 us (3%)
  local copies, waits for them, and re-layouts  13.7 us (3%)
    reduce_scatter x1, waiting for transfers between devices, body(): lax.psum_scatter(totals.reshape(6, -1), 'gx', scatter_dimension=1, tiled=...  144 us
    reduce_sum x16, other arithmetic, tile_rates(): jnp.sum(h * along_second * turn_first[k] - f * spin[k], axis=0)  127 us
    all_gather x1, waiting for transfers between devices, body(): lax.all_gather(resident, 'gx', axis=1, tiled=True).reshape(7, -1, BS)  86.2 us
    psum x1, waiting for transfers between devices, body(): rates = lax.psum(share, 'gy')  49.7 us
  transfers between devices with their start and end apart: 3, of which 3 were waited for; matrix products, arithmetic and copies ran while one was open for 1% of the time, Pallas kernels for 0%

commit v1 on v0

v1 whole, which is shorter than its diff:
```python
import functools

import jax
import jax.numpy as jnp
from jax import lax
from jax.experimental import pallas as pl
from jax.experimental.pallas import tpu as pltpu
from jax.sharding import PartitionSpec as P

BS = 1024
TILES_DEV = 8
BLK_DEV = 4
N_Z, N_X, N_CORE, N_Y = 8, 4, 2, 4
TEAM = N_CORE * N_Y
SLOTS = 2 * TILES_DEV
NB = 256
ROW = BLK_DEV * N_CORE * N_X
LANES = 128
MESH = pl.DeviceIdType.MESH

inv_four_pi = 0.07957747154594767
f32, bf16 = jnp.float32, jnp.bfloat16
NT = (((1,), (1,)), ((), ()))
NN = (((1,), (0,)), ((), ()))


def split3(a):
    hi = a.astype(bf16)
    rest = a - hi.astype(f32)
    mid = rest.astype(bf16)
    lo = (rest - mid.astype(f32)).astype(bf16)
    return hi, mid, lo


def split2(v):
    hi = v.astype(bf16)
    return hi, (v - hi.astype(f32)).astype(bf16)


def cross_rows(a, b):
    a0, a1, a2 = (a[k : k + 1] for k in range(3))
    b0, b1, b2 = (b[k : k + 1] for k in range(3))
    return jnp.concatenate([a1 * b2 - a2 * b1, a2 * b0 - a0 * b2, a0 * b1 - a1 * b0], 0)


def moments(x, w):
    base = jnp.concatenate([w, cross_rows(x, w), jnp.zeros((2, w.shape[1]), f32)], 0)
    parts = [base] + [x[k : k + 1] * base for k in range(3)]
    full = split3(jnp.concatenate(parts, 0))
    return jnp.concatenate([s[:8] for s in full], 0), jnp.concatenate(full, 0)


def gains(x, w, a, s):
    a = a[0:8] + (a[8:16] + a[16:24])
    s = s[0:32] + (s[32:64] + s[64:96])
    along = x[0:1] * w[0:1] + x[1:2] * w[1:2] + x[2:3] * w[2:3]
    t = along * s[0:8] - (w[0:1] * s[8:16] + w[1:2] * s[16:24] + w[2:3] * s[24:32])
    vel = (cross_rows(x, a[0:3]) - a[3:6]) * -inv_four_pi
    turn = cross_rows(x, t[0:3]) - t[3:6]
    stretch = (3.0 * inv_four_pi) * turn - inv_four_pi * cross_rows(w, a[0:3])
    return vel, stretch


def tile_rates(first, second, piece):
    n = first.shape[1]
    total = jnp.sum(first[0:3], axis=1, keepdims=True) + jnp.sum(second[0:3], axis=1, keepdims=True)
    centre = total * (0.5 / n)
    xp, xq = first[0:3] - centre, second[0:3] - centre
    wp, wq = first[3:6], second[3:6]
    sp, sq = 0.5 * first[6:7] * first[6:7], 0.5 * second[6:7] * second[6:7]
    bp, mp = moments(xp, wp)
    bq, mq = moments(xq, wq)
    cols = jnp.transpose(jnp.concatenate([first[0:3], sp, first[4:8]], 0))
    aq = jnp.zeros((24, n), f32)
    hq = jnp.zeros((96, n), f32)
    ap, hp = [], []
    dot = functools.partial(lax.dot_general, preferred_element_type=f32)
    for s in range(0, n, piece):
        cs = cols[s : s + piece]
        r = [cs[:, k : k + 1] - second[k : k + 1] for k in range(3)]
        g = r[0] * r[0] + r[1] * r[1] + r[2] * r[2] + (cs[:, 3:4] + sq)
        q = lax.rsqrt(g)
        q2 = q * q
        f = q2 * q
        h = f * q2
        fh, fl = split2(f)
        hh, hl = split2(h)
        ap.append(dot(fh, bq, NT) + dot(fl, bq, NT))
        hp.append(dot(hh, mq, NT) + dot(hl, mq, NT))
        bps, mps = bp[:, s : s + piece], mp[:, s : s + piece]
        aq = aq + (dot(bps, fh, NN) + dot(bps, fl, NN))
        hq = hq + (dot(mps, hh, NN) + dot(mps, hl, NN))
    ap, hp = jnp.transpose(jnp.concatenate(ap, 0)), jnp.transpose(jnp.concatenate(hp, 0))
    return gains(xp, wp, ap, hp) + gains(xq, wq, aq, hq)


def pairs_kernel(in_ref, out_ref):
    def step(t, _):
        def rows(s):
            return jnp.concatenate([in_ref[e, s] for e in range(TEAM)], 1)

        v1, s1, v2, s2 = tile_rates(rows(2 * t), rows(2 * t + 1), 128)
        for s, v, st in ((2 * t, v1, s1), (2 * t + 1, v2, s2)):
            full = jnp.concatenate([v, st, jnp.zeros((2, v.shape[1]), f32)], 0)
            for e in range(TEAM):
                out_ref[e, s] = full[:, LANES * e : LANES * (e + 1)]
        return 0

    lax.fori_loop(0, TILES_DEV, step, 0)


def pairs(blocks):
    return pl.pallas_call(
        pairs_kernel,
        out_shape=jax.ShapeDtypeStruct((TEAM, SLOTS, 8, LANES), f32),
        in_specs=[pl.BlockSpec(memory_space=pltpu.VMEM)],
        out_specs=pl.BlockSpec(memory_space=pltpu.VMEM),
        compiler_params=pltpu.CompilerParams(vmem_limit_bytes=48 * 2**20),
    )(blocks)


def place():
    gx, y = lax.axis_index("gx"), lax.axis_index("gy")
    core = lax.rem(gx, 2)
    x = lax.rem(gx // 2, N_X)
    z = gx // (2 * N_X)
    return z, x, core, y


def gx_of(z, x, core):
    return (z * N_X + x) * 2 + core


def wrap(v, n):
    return lax.rem(v + n, n)


X_OFFSETS = [(0, 1), (1, 0), (3, 0), (1, 1), (3, 1), (2, 0), (2, 1)]
TEAM_OFFSETS = [(0, 1), (1, 0), (3, 0), (1, 1), (3, 1), (2, 0), (2, 1)]


def flip(core, d):
    return core if d == 0 else 1 - core


def greet(z, x, core, y):
    barrier = pltpu.get_barrier_semaphore()
    there = [(gx_of(z, wrap(x + dx, N_X), flip(core, dc)), y) for dx, dc in X_OFFSETS]
    there += [(gx_of(wrap(z + dz, N_Z), x, core), y) for dz in (1, -1)]
    there += [(gx_of(z, x, flip(core, dc)), wrap(y + dy, N_Y)) for dy, dc in TEAM_OFFSETS if dy]
    for device in there:
        pl.semaphore_signal(barrier, inc=1, device_id=device, device_id_type=MESH)
    pl.semaphore_wait(barrier, len(there))


def remote(src, dst, send, recv, device):
    return pltpu.make_async_remote_copy(
        src_ref=src, dst_ref=dst, send_sem=send, recv_sem=recv, device_id=device, device_id_type=MESH
    )


def gather_kernel(
    ids_ref, pos_ref, str_ref, rad_ref, out_ref, own, grid, pack, xs, xr, zs, zr, ts, tr
):
    z, x, core, y = place()
    gx = gx_of(z, x, core)
    me = core * N_Y + y
    for c in range(N_CORE):
        for b in range(BLK_DEV):
            at = pl.ds(pl.multiple_of(b * BS + (c * N_Y + y) * LANES, LANES), LANES)
            own[c, b] = jnp.zeros((8, LANES), f32)
            own[c, b, 0:3, :] = pos_ref[:, at]
            own[c, b, 3:6, :] = str_ref[:, at]
            own[c, b, 6:7, :] = rad_ref[:, at]
    greet(z, x, core, y)

    def mine(first):
        return grid.at[pl.ds(first * BLK_DEV, BLK_DEV)]

    copies = []
    for i, (dx, dc) in enumerate(X_OFFSETS):
        there = flip(core, dc)
        to = (gx_of(z, wrap(x + dx, N_X), there), y)
        copy = remote(own.at[there], mine(gx), xs.at[i], xr.at[i], to)
        copy.start()
        copies.append(copy)
    for b in range(BLK_DEV):
        grid[gx * BLK_DEV + b] = own[core, b]

    def piece(row, u):
        return grid.at[pl.ds((row * N_X + wrap(x + u, N_X)) * 2 * BLK_DEV, 2 * BLK_DEV)]

    def along(way, s, u):
        row = wrap(z - s, N_Z) if way == 0 else wrap(z + s, N_Z)
        to = (gx_of(wrap(z + (1 if way == 0 else -1), N_Z), x, core), y)
        return remote(piece(row, u), piece(row, u), zs.at[way, s, u], zr.at[way, s, u], to)

    def arrived(way, s, u):
        row = wrap(z - s - 1, N_Z) if way == 0 else wrap(z + s + 1, N_Z)
        return remote(
            piece(row, u), piece(row, u), zs.at[way, s, u], zr.at[way, s, u], (gx, wrap(y + 1, N_Y))
        )

    def x_arrived(i):
        dx, dc = X_OFFSETS[i]
        source = gx_of(z, wrap(x - dx, N_X), flip(core, dc))
        remote(own.at[0], mine(source), xs.at[i], xr.at[i], (gx, wrap(y + 1, N_Y))).wait_recv()

    order = {0: [0], 3: [1, 3], 1: [2, 4], 2: [5, 6]}
    last = {0: (0, 1), 1: (2, 3)}
    sends = []
    for s in range(4):
        for u, needs in order.items():
            if s == 0:
                for i in needs:
                    x_arrived(i)
            for way in (0, 1):
                if s == 3 and u not in last[way]:
                    continue
                if s:
                    arrived(way, s - 1, u).wait_recv()
                copy = along(way, s, u)
                copy.start()
                sends.append(copy)
    for way in (0, 1):
        for u in range(4):
            if u not in last[way]:
                arrived(way, 2, u).wait_recv()
        for u in last[way]:
            arrived(way, 3, u).wait_recv()

    for i, (dy, dc) in enumerate(TEAM_OFFSETS):
        there_core, there_y = flip(core, dc), wrap(y + dy, N_Y)
        member = there_core * N_Y + there_y
        for k in range(SLOTS):
            pack[i, k] = grid[ids_ref[member * SLOTS + k]]
        copy = remote(
            pack.at[i], out_ref.at[me], ts.at[i], tr.at[i], (gx_of(z, x, there_core), there_y)
        )
        copy.start()
        sends.append(copy)
    for k in range(SLOTS):
        out_ref[me, k] = grid[ids_ref[me * SLOTS + k]]
    for copy in copies + sends:
        copy.wait_send()
    for i, (dy, dc) in enumerate(TEAM_OFFSETS):
        member = flip(core, dc) * N_Y + wrap(y - dy, N_Y)
        remote(
            pack.at[i], out_ref.at[member], ts.at[i], tr.at[i], (gx, wrap(y + 1, N_Y))
        ).wait_recv()


def gather(ids, positions, strengths, radii):
    vmem = pl.BlockSpec(memory_space=pltpu.VMEM)
    dma = pltpu.SemaphoreType.DMA
    return pl.pallas_call(
        gather_kernel,
        out_shape=jax.ShapeDtypeStruct((TEAM, SLOTS, 8, LANES), f32),
        in_specs=[pl.BlockSpec(memory_space=pltpu.SMEM)] + [vmem] * 3,
        out_specs=vmem,
        scratch_shapes=[
            pltpu.VMEM((N_CORE, BLK_DEV, 8, LANES), f32),
            pltpu.VMEM((NB, 8, LANES), f32),
            pltpu.VMEM((7, SLOTS, 8, LANES), f32),
            dma((7,)),
            dma((7,)),
            dma((2, 4, 4)),
            dma((2, 4, 4)),
            dma((7,)),
            dma((7,)),
        ],
        compiler_params=pltpu.CompilerParams(
            collective_id=0, has_side_effects=True, vmem_limit_bytes=32 * 2**20
        ),
    )(ids, positions, strengths, radii)


def reduce_kernel(
    at_ref, part_ref, vel_ref, str_ref, team, dense, zin, xin, fin, ts, tr, zs, zr, xs, xr, ys, yr
):
    z, x, core, y = place()
    gx = gx_of(z, x, core)
    me = core * N_Y + y
    other = (gx, wrap(y + 1, N_Y))
    greet(z, x, core, y)
    sends = []
    for i, (dy, dc) in enumerate(TEAM_OFFSETS):
        there_core, there_y = flip(core, dc), wrap(y + dy, N_Y)
        copy = remote(
            part_ref.at[there_core * N_Y + there_y],
            team.at[pl.ds(me * (SLOTS + 1), SLOTS)],
            ts.at[i],
            tr.at[i],
            (gx_of(z, x, there_core), there_y),
        )
        copy.start()
        sends.append(copy)
    for m in range(TEAM):
        team[m * (SLOTS + 1) + SLOTS] = jnp.zeros((8, LANES), f32)
    for k in range(SLOTS):
        team[me * (SLOTS + 1) + k] = part_ref[me, k]
    for i, (dy, dc) in enumerate(TEAM_OFFSETS):
        member = flip(core, dc) * N_Y + wrap(y - dy, N_Y)
        remote(
            part_ref.at[0], team.at[pl.ds(member * (SLOTS + 1), SLOTS)], ts.at[i], tr.at[i], other
        ).wait_recv()

    def fill(row, u):
        first = (row * N_X + wrap(x + u, N_X)) * 2 * BLK_DEV

        def one(j, _):
            b = first + j
            terms = [team[at_ref[m * NB + b]] for m in range(TEAM)]
            while len(terms) > 1:
                terms = [terms[k] + terms[k + 1] for k in range(0, len(terms), 2)]
            dense[b] = terms[0]
            return 0

        lax.fori_loop(0, 2 * BLK_DEV, one, 0, unroll=True)

    def piece(row, u):
        return dense.at[pl.ds((row * N_X + wrap(x + u, N_X)) * 2 * BLK_DEV, 2 * BLK_DEV)]

    def add(row, u, way, s):
        first = (row * N_X + wrap(x + u, N_X)) * 2 * BLK_DEV
        for j in range(2 * BLK_DEV):
            dense[first + j] = dense[first + j] + zin[way, s, u, j]

    def along(way, s, u):
        row = wrap(z + 4 - s, N_Z) if way == 0 else wrap(z - 4 + s, N_Z)
        to = (gx_of(wrap(z + (1 if way == 0 else -1), N_Z), x, core), y)
        return remote(piece(row, u), zin.at[way, s, u], zs.at[way, s, u], zr.at[way, s, u], to)

    def arrived(way, s, u):
        return remote(
            piece(z, u), zin.at[way, s, u], zs.at[way, s, u], zr.at[way, s, u], other
        ).wait_recv()

    first = {0: (0, 1), 1: (2, 3)}
    for s in range(4):
        if s == 0:
            for u in range(4):
                fill(wrap(z + 4, N_Z), u)
                way = 0 if u in first[0] else 1
                copy = along(way, 0, u)
                copy.start()
                sends.append(copy)
            continue
        for u in (2, 3, 0, 1):
            for way in (0, 1):
                row = wrap(z + 4 - s, N_Z) if way == 0 else wrap(z - 4 + s, N_Z)
                fill(row, u)
                if s > 1 or u in first[way]:
                    arrived(way, s - 1, u)
                    add(row, u, way, s - 1)
                copy = along(way, s, u)
                copy.start()
                sends.append(copy)
    for u in range(4):
        fill(z, u)
        for way in (0, 1):
            arrived(way, 3, u)
            add(z, u, way, 3)

    def home(first):
        return dense.at[pl.ds(first * BLK_DEV, BLK_DEV)]

    for i, (dx, dc) in enumerate(X_OFFSETS):
        there = gx_of(z, wrap(x + dx, N_X), flip(core, dc))
        copy = remote(home(there), xin.at[i], xs.at[i], xr.at[i], (there, y))
        copy.start()
        sends.append(copy)
    for i in range(7):
        remote(home(gx), xin.at[i], xs.at[i], xr.at[i], other).wait_recv()
    by_core = {d: [i for i, (_, dc) in enumerate(X_OFFSETS) if dc == d] for d in (0, 1)}
    for b in range(BLK_DEV):
        a = [xin[i, b] for i in by_core[0]]
        fin[0, core, b] = (dense[gx * BLK_DEV + b] + a[0]) + (a[1] + a[2])
        a = [xin[i, b] for i in by_core[1]]
        fin[0, 1 - core, b] = (a[0] + a[1]) + (a[2] + a[3])
    for i, dy in enumerate((1, 3, 2)):
        copy = remote(fin.at[0], fin.at[i + 1], ys.at[i], yr.at[i], (gx, wrap(y + dy, N_Y)))
        copy.start()
        sends.append(copy)

    def write(slot, there_y):
        for c in range(N_CORE):
            for b in range(BLK_DEV):
                at = pl.ds(pl.multiple_of(b * BS + (c * N_Y + there_y) * LANES, LANES), LANES)
                full = fin[slot, c, b]
                vel_ref[:, at] = full[0:3]
                str_ref[:, at] = full[3:6]

    write(0, y)
    for i, dy in enumerate((1, 3, 2)):
        remote(fin.at[0], fin.at[i + 1], ys.at[i], yr.at[i], other).wait_recv()
        write(i + 1, wrap(y - dy, N_Y))
    for copy in sends:
        copy.wait_send()


def reduce(at, partials):
    vmem = pl.BlockSpec(memory_space=pltpu.VMEM)
    dma = pltpu.SemaphoreType.DMA
    out = jax.ShapeDtypeStruct((3, BLK_DEV * BS), f32)
    return pl.pallas_call(
        reduce_kernel,
        out_shape=(out, out),
        in_specs=[pl.BlockSpec(memory_space=pltpu.SMEM), vmem],
        out_specs=(vmem, vmem),
        scratch_shapes=[
            pltpu.VMEM((TEAM * (SLOTS + 1), 8, LANES), f32),
            pltpu.VMEM((NB, 8, LANES), f32),
            pltpu.VMEM((2, 4, 4, 2 * BLK_DEV, 8, LANES), f32),
            pltpu.VMEM((7, BLK_DEV, 8, LANES), f32),
            pltpu.VMEM((4, N_CORE, BLK_DEV, 8, LANES), f32),
            dma((7,)),
            dma((7,)),
            dma((2, 4, 4)),
            dma((2, 4, 4)),
            dma((7,)),
            dma((7,)),
            dma((3,)),
            dma((3,)),
        ],
        compiler_params=pltpu.CompilerParams(
            collective_id=1, has_side_effects=True, vmem_limit_bytes=32 * 2**20
        ),
    )(at, partials)


def body(positions, strengths, core_radii, tile_pairs, block_home):
    chip = lax.axis_index("gx") // 2
    teams = tile_pairs.reshape(N_Z * N_X, TEAM * SLOTS)
    logical = lax.dynamic_index_in_dim(teams, chip, 0, keepdims=False)
    blocks = jnp.arange(NB, dtype=jnp.int32)
    match = logical[:, None] == blocks
    stored = jnp.sum(jnp.where(match, block_home, 0), axis=1)
    slot = jnp.arange(SLOTS, dtype=jnp.int32)[None, :, None]
    named = stored.reshape(TEAM, SLOTS, 1) == blocks
    at = jnp.min(jnp.where(named, slot, SLOTS), axis=1)
    at = at + (SLOTS + 1) * jnp.arange(TEAM, dtype=jnp.int32)[:, None]
    own_blocks = gather(stored, positions, strengths, core_radii[None, :])
    return reduce(at.reshape(-1), pairs(own_blocks))


def solution(mesh):
    return jax.shard_map(
        body,
        mesh=mesh,
        in_specs=(P(None, "gx"), P(None, "gx"), P("gx"), P(), P()),
        out_specs=(P(None, "gx"), P(None, "gx")),
        check_vma=False,
    )
```

time: 445 us -> 114 us (0.26)
  waiting for transfers between devices: 280 us -> 0 us
  other arithmetic: 134 us -> 0.37 us
  Pallas kernels: 0 us -> 108 us
  between operations: 13.9 us -> 0.74 us
  local copies, waits for them, and re-layouts: 13.7 us -> 3.7 us
    reduce_scatter x1 -> x0, waiting for transfers between devices: 144 us -> none  [body(): lax.psum_scatter(totals.reshape(6, -1), 'gx', scatter_dimension=1, tiled=...]
    reduce_sum x17 -> x1, other arithmetic: 128 us -> 0.17 us  [body(): stored = jnp.sum(jnp.where(match, block_home, 0), axis=1)]
    pallas_call x0 -> x3, Pallas kernels: none -> 108 us  [the longest x1 39.1 us: pairs(): pl.pallas_call(pairs_kernel, out_shape=jax.ShapeDtypeStruct((TEAM, SLOTS,...]
    all_gather x1 -> x0, waiting for transfers between devices: 86.2 us -> none  [body(): lax.all_gather(resident, 'gx', axis=1, tiled=True).reshape(7, -1, BS)]
    psum x1 -> x0, waiting for transfers between devices: 49.7 us -> none  [body(): rates = lax.psum(share, 'gy')]
  transfers between devices with their start and end apart: 3 -> 0, of which waited for: 3 -> 0; matrix products, arithmetic and copies ran while one was open for 1% -> 0% of each run, Pallas kernels for 0% -> 0%
where the time goes in v1:
time: 114 us; the launch traced here: 113 us
  Pallas kernels  108 us (95%)
  local copies, waits for them, and re-layouts  3.7 us (3%)
    pallas_call x1, Pallas kernels, pairs(): pl.pallas_call(pairs_kernel, out_shape=jax.ShapeDtypeStruct((TEAM, SLOTS,...  39.1 us
    pallas_call x1, Pallas kernels, reduce(): pl.pallas_call(reduce_kernel, out_shape=(out, out), in_specs=[pl.BlockSpe...  34.8 us
    pallas_call x1, Pallas kernels, gather(): pl.pallas_call(gather_kernel, out_shape=jax.ShapeDtypeStruct((TEAM, SLOTS...  34.5 us
    unnamed x12, local copies, waits for them, and re-layouts  3.14 us

profile of v1, /device:TPU:1, one launch (start us, length us, event | category | flops | bytes accessed | tf_op | source)
XLA Modules:
  0.0 113.3 jit_solution(17610015591338177715)
XLA Ops:
  0.6 1.1 copy.8
  1.7 0.0 copy-start.3
  1.7 0.0 copy-start.1
  1.7 0.5 reshape.20
  2.2 0.0 copy-start
  2.2 0.2 copy-done.3
  2.4 0.2 select_reduce_fusion.1.ids_ref
  2.6 0.1 eq.34
  2.6 0.1 select_reduce_fusion
  2.8 0.0 copy-start.2
  2.8 0.1 add_bitcast_fusion
  2.9 0.0 copy-done.1
  2.9 0.2 copy-done
  3.1 0.5 copy-done.2
  3.5 34.5 %shard_map.68.in_ref = f32[8,16,8,128]{3,2,1,0:T(8,128)S(1)} custom-call(s32[128]{0:T(128)S(1)} %select_reduce_fusion.1.ids_ref, f32[3,4096]{1,0:T(4,128)S(1)} %copy-done, f32[3,4096]{1,0:T(4,128)S(1)} %copy-done.1, f32[1,4096]{1,0:T(1,128)S(1)} %bitcast.7), custom_call_target="tpu_custom_call" | custom-call | tf_op jit(solution)/shard_map/pallas_call | solution.py:256
  38.1 39.1 %shard_map.69.part_ref = f32[8,16,8,128]{3,2,1,0:T(8,128)S(1)} custom-call(f32[8,16,8,128]{3,2,1,0:T(8,128)S(1)} %shard_map.68.in_ref), custom_call_target="tpu_custom_call" | custom-call | tf_op jit(solution)/shard_map/pallas_call | solution.py:113
  77.2 34.8 %shard_map.70 = (f32[3,4096]{1,0:T(4,128)S(1)}, f32[3,4096]{1,0:T(4,128)S(1)}) custom-call(s32[2048]{0:T(1024)S(1)} %bitcast.6, f32[8,16,8,128]{3,2,1,0:T(8,128)S(1)} %shard_map.69.part_ref), custom_call_target="tpu_custom_call" | custom-call | tf_op jit(solution)/shard_map/pallas_call | solution.py:406
  112.0 0.6 copy.12
  112.6 0.6 copy.13
  (3 shorter events, 0.0 us)
Async XLA Ops:
  1.7 0.7 copy-start.3
  1.7 1.2 %copy-start.1 = (f32[3,4096]{1,0:T(4,128)S(1)}, f32[3,4096]{1,0:T(4,128)}, u32[]{:S(2)}) copy-start(f32[3,4096]{1,0:T(4,128)} %str_ref.1) | copy-start | bytes 147460
  2.2 0.8 copy-start
  2.8 0.7 copy-start.2

commit v2 on v1

--- a/solution.py
+++ b/solution.py
@@ -94,31 +94,6 @@
     return gains(xp, wp, ap, hp) + gains(xq, wq, aq, hq)
 
 
-def pairs_kernel(in_ref, out_ref):
-    def step(t, _):
-        def rows(s):
-            return jnp.concatenate([in_ref[e, s] for e in range(TEAM)], 1)
-
-        v1, s1, v2, s2 = tile_rates(rows(2 * t), rows(2 * t + 1), 128)
-        for s, v, st in ((2 * t, v1, s1), (2 * t + 1, v2, s2)):
-            full = jnp.concatenate([v, st, jnp.zeros((2, v.shape[1]), f32)], 0)
-            for e in range(TEAM):
-                out_ref[e, s] = full[:, LANES * e : LANES * (e + 1)]
-        return 0
-
-    lax.fori_loop(0, TILES_DEV, step, 0)
-
-
-def pairs(blocks):
-    return pl.pallas_call(
-        pairs_kernel,
-        out_shape=jax.ShapeDtypeStruct((TEAM, SLOTS, 8, LANES), f32),
-        in_specs=[pl.BlockSpec(memory_space=pltpu.VMEM)],
-        out_specs=pl.BlockSpec(memory_space=pltpu.VMEM),
-        compiler_params=pltpu.CompilerParams(vmem_limit_bytes=48 * 2**20),
-    )(blocks)
-
-
 def place():
     gx, y = lax.axis_index("gx"), lax.axis_index("gy")
     core = lax.rem(gx, 2)
@@ -159,11 +134,14 @@
     )
 
 
-def gather_kernel(
-    ids_ref, pos_ref, str_ref, rad_ref, out_ref, own, grid, pack, xs, xr, zs, zr, ts, tr
+def kernel(
+    ids_ref, at_ref, pos_ref, str_ref, rad_ref, vel_out, str_out,
+    own, grid, pack, named, part, team, dense, zin, xin, fin,
+    gxs, gxr, gzs, gzr, ts, tr, ps, pr, zs, zr, xs, xr, ys, yr,
 ):
     z, x, core, y = place()
     gx = gx_of(z, x, core)
+    other = (gx, wrap(y + 1, N_Y))
     me = core * N_Y + y
     for c in range(N_CORE):
         for b in range(BLK_DEV):
@@ -181,30 +159,30 @@
     for i, (dx, dc) in enumerate(X_OFFSETS):
         there = flip(core, dc)
         to = (gx_of(z, wrap(x + dx, N_X), there), y)
-        copy = remote(own.at[there], mine(gx), xs.at[i], xr.at[i], to)
+        copy = remote(own.at[there], mine(gx), gxs.at[i], gxr.at[i], to)
         copy.start()
         copies.append(copy)
     for b in range(BLK_DEV):
         grid[gx * BLK_DEV + b] = own[core, b]
 
-    def piece(row, u):
+    def part_of(row, u):
         return grid.at[pl.ds((row * N_X + wrap(x + u, N_X)) * 2 * BLK_DEV, 2 * BLK_DEV)]
 
-    def along(way, s, u):
+    def onward(way, s, u):
         row = wrap(z - s, N_Z) if way == 0 else wrap(z + s, N_Z)
         to = (gx_of(wrap(z + (1 if way == 0 else -1), N_Z), x, core), y)
-        return remote(piece(row, u), piece(row, u), zs.at[way, s, u], zr.at[way, s, u], to)
-
-    def arrived(way, s, u):
+        return remote(part_of(row, u), part_of(row, u), gzs.at[way, s, u], gzr.at[way, s, u], to)
+
+    def came(way, s, u):
         row = wrap(z - s - 1, N_Z) if way == 0 else wrap(z + s + 1, N_Z)
         return remote(
-            piece(row, u), piece(row, u), zs.at[way, s, u], zr.at[way, s, u], (gx, wrap(y + 1, N_Y))
+            part_of(row, u), part_of(row, u), gzs.at[way, s, u], gzr.at[way, s, u], (gx, wrap(y + 1, N_Y))
         )
 
-    def x_arrived(i):
+    def x_came(i):
         dx, dc = X_OFFSETS[i]
         source = gx_of(z, wrap(x - dx, N_X), flip(core, dc))
-        remote(own.at[0], mine(source), xs.at[i], xr.at[i], (gx, wrap(y + 1, N_Y))).wait_recv()
+        remote(own.at[0], mine(source), gxs.at[i], gxr.at[i], (gx, wrap(y + 1, N_Y))).wait_recv()
 
     order = {0: [0], 3: [1, 3], 1: [2, 4], 2: [5, 6]}
     last = {0: (0, 1), 1: (2, 3)}
@@ -213,97 +191,101 @@
         for u, needs in order.items():
             if s == 0:
                 for i in needs:
-                    x_arrived(i)
+                    x_came(i)
             for way in (0, 1):
                 if s == 3 and u not in last[way]:
                     continue
                 if s:
-                    arrived(way, s - 1, u).wait_recv()
-                copy = along(way, s, u)
+                    came(way, s - 1, u).wait_recv()
+                copy = onward(way, s, u)
                 copy.start()
                 sends.append(copy)
     for way in (0, 1):
         for u in range(4):
             if u not in last[way]:
-                arrived(way, 2, u).wait_recv()
+                came(way, 2, u).wait_recv()
         for u in last[way]:
-            arrived(way, 3, u).wait_recv()
-
-    for i, (dy, dc) in enumerate(TEAM_OFFSETS):
+            came(way, 3, u).wait_recv()
+
+    def two(t):
+        return pl.ds(pl.multiple_of(2 * t, 2), 2)
+
+    def mate(i):
+        dy, dc = TEAM_OFFSETS[i]
         there_core, there_y = flip(core, dc), wrap(y + dy, N_Y)
-        member = there_core * N_Y + there_y
-        for k in range(SLOTS):
-            pack[i, k] = grid[ids_ref[member * SLOTS + k]]
-        copy = remote(
-            pack.at[i], out_ref.at[me], ts.at[i], tr.at[i], (gx_of(z, x, there_core), there_y)
+        return there_core * N_Y + there_y, (gx_of(z, x, there_core), there_y)
+
+    def mate_from(i):
+        dy, dc = TEAM_OFFSETS[i]
+        return flip(core, dc) * N_Y + wrap(y - dy, N_Y)
+
+    def ask(i, t):
+        return remote(
+            pack.at[i, two(t)], named.at[me, two(t)], ts.at[i, t], tr.at[i, t], mate(i)[1]
         )
-        copy.start()
-        sends.append(copy)
-    for k in range(SLOTS):
-        out_ref[me, k] = grid[ids_ref[me * SLOTS + k]]
-    for copy in copies + sends:
-        copy.wait_send()
-    for i, (dy, dc) in enumerate(TEAM_OFFSETS):
-        member = flip(core, dc) * N_Y + wrap(y - dy, N_Y)
-        remote(
-            pack.at[i], out_ref.at[member], ts.at[i], tr.at[i], (gx, wrap(y + 1, N_Y))
-        ).wait_recv()
-
-
-def gather(ids, positions, strengths, radii):
-    vmem = pl.BlockSpec(memory_space=pltpu.VMEM)
-    dma = pltpu.SemaphoreType.DMA
-    return pl.pallas_call(
-        gather_kernel,
-        out_shape=jax.ShapeDtypeStruct((TEAM, SLOTS, 8, LANES), f32),
-        in_specs=[pl.BlockSpec(memory_space=pltpu.SMEM)] + [vmem] * 3,
-        out_specs=vmem,
-        scratch_shapes=[
-            pltpu.VMEM((N_CORE, BLK_DEV, 8, LANES), f32),
-            pltpu.VMEM((NB, 8, LANES), f32),
-            pltpu.VMEM((7, SLOTS, 8, LANES), f32),
-            dma((7,)),
-            dma((7,)),
-            dma((2, 4, 4)),
-            dma((2, 4, 4)),
-            dma((7,)),
-            dma((7,)),
-        ],
-        compiler_params=pltpu.CompilerParams(
-            collective_id=0, has_side_effects=True, vmem_limit_bytes=32 * 2**20
-        ),
-    )(ids, positions, strengths, radii)
-
-
-def reduce_kernel(
-    at_ref, part_ref, vel_ref, str_ref, team, dense, zin, xin, fin, ts, tr, zs, zr, xs, xr, ys, yr
-):
-    z, x, core, y = place()
-    gx = gx_of(z, x, core)
-    me = core * N_Y + y
-    other = (gx, wrap(y + 1, N_Y))
-    greet(z, x, core, y)
-    sends = []
-    for i, (dy, dc) in enumerate(TEAM_OFFSETS):
-        there_core, there_y = flip(core, dc), wrap(y + dy, N_Y)
-        copy = remote(
-            part_ref.at[there_core * N_Y + there_y],
-            team.at[pl.ds(me * (SLOTS + 1), SLOTS)],
-            ts.at[i],
-            tr.at[i],
-            (gx_of(z, x, there_core), there_y),
+
+    def give(i, t):
+        member, to = mate(i)
+        return remote(
+            part.at[member, two(t)],
+            team.at[pl.ds(me * (SLOTS + 1) + 2 * t, 2)],
+            ps.at[i, t],
+            pr.at[i, t],
+            to,
         )
-        copy.start()
-        sends.append(copy)
+
+    def send_tile(t, _):
+        for i in range(7):
+            member = mate(i)[0]
+            for k in (2 * t, 2 * t + 1):
+                pack[i, k] = grid[ids_ref[member * SLOTS + k]]
+            ask(i, t).start()
+        for k in (2 * t, 2 * t + 1):
+            named[me, k] = grid[ids_ref[me * SLOTS + k]]
+        return 0
+
+    lax.fori_loop(0, TILES_DEV, send_tile, 0)
     for m in range(TEAM):
         team[m * (SLOTS + 1) + SLOTS] = jnp.zeros((8, LANES), f32)
-    for k in range(SLOTS):
-        team[me * (SLOTS + 1) + k] = part_ref[me, k]
-    for i, (dy, dc) in enumerate(TEAM_OFFSETS):
-        member = flip(core, dc) * N_Y + wrap(y - dy, N_Y)
-        remote(
-            part_ref.at[0], team.at[pl.ds(member * (SLOTS + 1), SLOTS)], ts.at[i], tr.at[i], other
-        ).wait_recv()
+
+    def one_tile(t, _):
+        for i in range(7):
+            member = mate_from(i)
+            remote(
+                pack.at[i, two(t)], named.at[member, two(t)], ts.at[i, t], tr.at[i, t], other
+            ).wait_recv()
+
+        def rows(s):
+            return jnp.concatenate([named[e, s] for e in range(TEAM)], 1)
+
+        v1, s1, v2, s2 = tile_rates(rows(2 * t), rows(2 * t + 1), 128)
+        for s, v, st in ((2 * t, v1, s1), (2 * t + 1, v2, s2)):
+            full = jnp.concatenate([v, st, jnp.zeros((2, v.shape[1]), f32)], 0)
+            for e in range(TEAM):
+                part[e, s] = full[:, LANES * e : LANES * (e + 1)]
+        for i in range(7):
+            give(i, t).start()
+        for k in (2 * t, 2 * t + 1):
+            team[me * (SLOTS + 1) + k] = part[me, k]
+        return 0
+
+    lax.fori_loop(0, TILES_DEV, one_tile, 0)
+
+    def settle(t, _):
+        for i in range(7):
+            ask(i, t).wait_send()
+            give(i, t).wait_send()
+            member = mate_from(i)
+            remote(
+                part.at[0, two(t)],
+                team.at[pl.ds(member * (SLOTS + 1) + 2 * t, 2)],
+                ps.at[i, t],
+                pr.at[i, t],
+                other,
+            ).wait_recv()
+        return 0
+
+    lax.fori_loop(0, TILES_DEV, settle, 0)
 
     def fill(row, u):
         first = (row * N_X + wrap(x + u, N_X)) * 2 * BLK_DEV
@@ -336,12 +318,12 @@
             piece(z, u), zin.at[way, s, u], zs.at[way, s, u], zr.at[way, s, u], other
         ).wait_recv()
 
-    first = {0: (0, 1), 1: (2, 3)}
+    early = {0: (0, 1), 1: (2, 3)}
     for s in range(4):
         if s == 0:
             for u in range(4):
                 fill(wrap(z + 4, N_Z), u)
-                way = 0 if u in first[0] else 1
+                way = 0 if u in early[0] else 1
                 copy = along(way, 0, u)
                 copy.start()
                 sends.append(copy)
@@ -350,7 +332,7 @@
             for way in (0, 1):
                 row = wrap(z + 4 - s, N_Z) if way == 0 else wrap(z - 4 + s, N_Z)
                 fill(row, u)
-                if s > 1 or u in first[way]:
+                if s > 1 or u in early[way]:
                     arrived(way, s - 1, u)
                     add(row, u, way, s - 1)
                 copy = along(way, s, u)
@@ -388,45 +370,45 @@
             for b in range(BLK_DEV):
                 at = pl.ds(pl.multiple_of(b * BS + (c * N_Y + there_y) * LANES, LANES), LANES)
                 full = fin[slot, c, b]
-                vel_ref[:, at] = full[0:3]
-                str_ref[:, at] = full[3:6]
+                vel_out[:, at] = full[0:3]
+                str_out[:, at] = full[3:6]
 
     write(0, y)
     for i, dy in enumerate((1, 3, 2)):
         remote(fin.at[0], fin.at[i + 1], ys.at[i], yr.at[i], other).wait_recv()
         write(i + 1, wrap(y - dy, N_Y))
-    for copy in sends:
+    for copy in copies + sends:
         copy.wait_send()
 
 
-def reduce(at, partials):
-    vmem = pl.BlockSpec(memory_space=pltpu.VMEM)
+def run(ids, at, positions, strengths, radii):
+    vmem, smem = pl.BlockSpec(memory_space=pltpu.VMEM), pl.BlockSpec(memory_space=pltpu.SMEM)
     dma = pltpu.SemaphoreType.DMA
     out = jax.ShapeDtypeStruct((3, BLK_DEV * BS), f32)
+    buffers = [
+        (N_CORE, BLK_DEV),
+        (NB,),
+        (7, SLOTS),
+        (TEAM, SLOTS),
+        (TEAM, SLOTS),
+        (TEAM * (SLOTS + 1),),
+        (NB,),
+        (2, 4, 4, 2 * BLK_DEV),
+        (7, BLK_DEV),
+        (4, N_CORE, BLK_DEV),
+    ]
+    counts = [(7,), (2, 4, 4), (7, TILES_DEV), (7, TILES_DEV), (2, 4, 4), (7,), (3,)]
     return pl.pallas_call(
-        reduce_kernel,
+        kernel,
         out_shape=(out, out),
-        in_specs=[pl.BlockSpec(memory_space=pltpu.SMEM), vmem],
+        in_specs=[smem, smem, vmem, vmem, vmem],
         out_specs=(vmem, vmem),
-        scratch_shapes=[
-            pltpu.VMEM((TEAM * (SLOTS + 1), 8, LANES), f32),
-            pltpu.VMEM((NB, 8, LANES), f32),
-            pltpu.VMEM((2, 4, 4, 2 * BLK_DEV, 8, LANES), f32),
-            pltpu.VMEM((7, BLK_DEV, 8, LANES), f32),
-            pltpu.VMEM((4, N_CORE, BLK_DEV, 8, LANES), f32),
-            dma((7,)),
-            dma((7,)),
-            dma((2, 4, 4)),
-            dma((2, 4, 4)),
-            dma((7,)),
-            dma((7,)),
-            dma((3,)),
-            dma((3,)),
-        ],
+        scratch_shapes=[pltpu.VMEM(b + (8, LANES), f32) for b in buffers]
+        + [dma(c) for c in counts for _ in range(2)],
         compiler_params=pltpu.CompilerParams(
-            collective_id=1, has_side_effects=True, vmem_limit_bytes=32 * 2**20
+            collective_id=0, has_side_effects=True, vmem_limit_bytes=48 * 2**20
         ),
-    )(at, partials)
+    )(ids, at, positions, strengths, radii)
 
 
 def body(positions, strengths, core_radii, tile_pairs, block_home):
@@ -440,8 +422,7 @@
     named = stored.reshape(TEAM, SLOTS, 1) == blocks
     at = jnp.min(jnp.where(named, slot, SLOTS), axis=1)
     at = at + (SLOTS + 1) * jnp.arange(TEAM, dtype=jnp.int32)[:, None]
-    own_blocks = gather(stored, positions, strengths, core_radii[None, :])
-    return reduce(at.reshape(-1), pairs(own_blocks))
+    return run(stored, at.reshape(-1), positions, strengths, core_radii[None, :])
 
 
 def solution(mesh):

time: 114 us -> 106 us (0.930)
  Pallas kernels: 108 us -> 101 us
    pallas_call x3 -> x1, Pallas kernels: 108 us -> 101 us  [run(): pl.pallas_call(kernel, out_shape=(out, out), in_specs=[smem, smem, vmem,...]
where the time goes in v2:
time: 106 us
  Pallas kernels  101 us (95%)
  local copies, waits for them, and re-layouts  3.7 us (3%)
    pallas_call x1, Pallas kernels, run(): pl.pallas_call(kernel, out_shape=(out, out), in_specs=[smem, smem, vmem,...  101 us
    unnamed x12, local copies, waits for them, and re-layouts  3.14 us

profile of v2, /device:TPU:1, one launch (start us, length us, event | category | flops | bytes accessed | tf_op | source)
XLA Modules:
  0.0 105.9 jit_solution(6236314687130784290)
XLA Ops:
  0.6 1.1 %copy.8 = s32[2048,2]{1,0:T(8,128)S(1)} copy(s32[2048,2]{0,1:T(2,128)} %param.8) | data formatting | bytes 32768 | tf_op args[3]
  1.7 0.0 copy-start.3
  1.7 0.0 copy-start.1
  1.7 0.5 reshape.20
  2.2 0.0 copy-start
  2.2 0.2 copy-done.3
  2.4 0.2 select_reduce_fusion.1.ids_ref
  2.6 0.1 eq.34
  2.6 0.1 select_reduce_fusion
  2.8 0.0 copy-start.2
  2.8 0.1 add_bitcast_fusion
  2.9 0.0 copy-done.1
  2.9 0.2 copy-done
  3.1 0.5 copy-done.2
  3.5 101.1 %shard_map.68 = (f32[3,4096]{1,0:T(4,128)S(1)}, f32[3,4096]{1,0:T(4,128)S(1)}) custom-call(s32[128]{0:T(128)S(1)} %select_reduce_fusion.1.ids_ref, s32[2048]{0:T(1024)S(1)} %bitcast.6, f32[3,4096]{1,0:T(4,128)S(1)} %copy-done, f32[3,4096]{1,0:T(4,128)S(1)} %copy-done.1, f32[1,4096]{1,0:T(1,128)S(1)} %bitcast.7), custom_call_target="tpu_custom_call" | custom-call | tf_op jit(solution)/shard_map/pallas_call | solution.py:401
  104.7 0.6 copy.12
  105.3 0.6 copy.13
  (3 shorter events, 0.0 us)
Async XLA Ops:
  1.7 0.7 copy-start.3
  1.7 1.2 %copy-start.1 = (f32[3,4096]{1,0:T(4,128)S(1)}, f32[3,4096]{1,0:T(4,128)}, u32[]{:S(2)}) copy-start(f32[3,4096]{1,0:T(4,128)} %str_ref.1) | copy-start | bytes 147460
  2.2 0.8 copy-start
  2.8 0.7 copy-start.2

commit v3 on v0

v3 whole, which is shorter than its diff:
```python
import functools

import jax
import jax.numpy as jnp
from jax import lax
from jax.experimental import pallas as pl
from jax.experimental.pallas import tpu as pltpu
from jax.sharding import PartitionSpec as P

BS = 1024
TILES_DEV = 8
BLK_DEV = 4
N_Z, N_X, N_CORE, N_Y = 8, 4, 2, 4
EIGHTHS = N_CORE * N_Y
TEAM = N_X * EIGHTHS
SENDERS = 3 * EIGHTHS
SLOTS = 2 * TILES_DEV
NB = 256
ROW = BLK_DEV * N_CORE * N_X
EARLY = TILES_DEV - 1
LANES = 128
MESH = pl.DeviceIdType.MESH

inv_four_pi = 0.07957747154594767
f32, bf16 = jnp.float32, jnp.bfloat16
NT = (((1,), (1,)), ((), ()))
NN = (((1,), (0,)), ((), ()))


def split3(a):
    hi = a.astype(bf16)
    rest = a - hi.astype(f32)
    mid = rest.astype(bf16)
    lo = (rest - mid.astype(f32)).astype(bf16)
    return hi, mid, lo


def split2(v):
    hi = v.astype(bf16)
    return hi, (v - hi.astype(f32)).astype(bf16)


def cross_rows(a, b):
    a0, a1, a2 = (a[k : k + 1] for k in range(3))
    b0, b1, b2 = (b[k : k + 1] for k in range(3))
    return jnp.concatenate([a1 * b2 - a2 * b1, a2 * b0 - a0 * b2, a0 * b1 - a1 * b0], 0)


def moments(x, w):
    base = jnp.concatenate([w, cross_rows(x, w), jnp.zeros((2, w.shape[1]), f32)], 0)
    parts = [base] + [x[k : k + 1] * base for k in range(3)]
    full = split3(jnp.concatenate(parts, 0))
    return jnp.concatenate([s[:8] for s in full], 0), jnp.concatenate(full, 0)


def gains(x, w, a, s):
    a = a[0:8] + (a[8:16] + a[16:24])
    s = s[0:32] + (s[32:64] + s[64:96])
    along = x[0:1] * w[0:1] + x[1:2] * w[1:2] + x[2:3] * w[2:3]
    t = along * s[0:8] - (w[0:1] * s[8:16] + w[1:2] * s[16:24] + w[2:3] * s[24:32])
    vel = (cross_rows(x, a[0:3]) - a[3:6]) * -inv_four_pi
    turn = cross_rows(x, t[0:3]) - t[3:6]
    stretch = (3.0 * inv_four_pi) * turn - inv_four_pi * cross_rows(w, a[0:3])
    return vel, stretch


def tile_rates(first, second, piece):
    n = first.shape[1]
    total = jnp.sum(first[0:3], axis=1, keepdims=True) + jnp.sum(second[0:3], axis=1, keepdims=True)
    centre = total * (0.5 / n)
    xp, xq = first[0:3] - centre, second[0:3] - centre
    wp, wq = first[3:6], second[3:6]
    sp, sq = 0.5 * first[6:7] * first[6:7], 0.5 * second[6:7] * second[6:7]
    bp, mp = moments(xp, wp)
    bq, mq = moments(xq, wq)
    cols = jnp.transpose(jnp.concatenate([first[0:3], sp, first[4:8]], 0))
    aq = jnp.zeros((24, n), f32)
    hq = jnp.zeros((96, n), f32)
    ap, hp = [], []
    dot = functools.partial(lax.dot_general, preferred_element_type=f32)
    for s in range(0, n, piece):
        cs = cols[s : s + piece]
        r = [cs[:, k : k + 1] - second[k : k + 1] for k in range(3)]
        g = r[0] * r[0] + r[1] * r[1] + r[2] * r[2] + (cs[:, 3:4] + sq)
        q = lax.rsqrt(g)
        q2 = q * q
        f = q2 * q
        h = f * q2
        fh, fl = split2(f)
        hh, hl = split2(h)
        ap.append(dot(fh, bq, NT) + dot(fl, bq, NT))
        hp.append(dot(hh, mq, NT) + dot(hl, mq, NT))
        bps, mps = bp[:, s : s + piece], mp[:, s : s + piece]
        aq = aq + (dot(bps, fh, NN) + dot(bps, fl, NN))
        hq = hq + (dot(mps, hh, NN) + dot(mps, hl, NN))
    ap, hp = jnp.transpose(jnp.concatenate(ap, 0)), jnp.transpose(jnp.concatenate(hp, 0))
    return gains(xp, wp, ap, hp) + gains(xq, wq, aq, hq)


def place():
    gx, y = lax.axis_index("gx"), lax.axis_index("gy")
    core = lax.rem(gx, 2)
    x = lax.rem(gx // 2, N_X)
    z = gx // (2 * N_X)
    return z, x, core, y


def gx_of(z, x, core):
    return (z * N_X + x) * 2 + core


def wrap(v, n):
    return lax.rem(v + n, n)


X_OFFSETS = [(2, 0), (2, 1), (1, 0), (3, 0), (1, 1), (3, 1), (0, 1)]
Z_OFFSETS = [4, 3, 5, 2, 6, 1, 7]


def flip(core, d):
    return lax.rem(core + d, 2)


def remote(src, dst, send, recv, device):
    return pltpu.make_async_remote_copy(
        src_ref=src, dst_ref=dst, send_sem=send, recv_sem=recv, device_id=device, device_id_type=MESH
    )


def kernel(
    ids_ref, keys_ref, pos_ref, str_ref, rad_ref, vel_out, str_out,
    own, grid, pack, named, part, team, pick, dense, zin, fin,
    xs, xr, gs, gr, ts, tr, ps, pr, zs, zr, fs, fr,
):
    z, x, core, y = place()
    gx = gx_of(z, x, core)
    me = x * EIGHTHS + core * N_Y + y
    other = (gx, wrap(y + 1, N_Y))
    active = x < 3

    def mate(i):
        tx, tc, ty = wrap(x + i // 8, N_X), flip(core, (i // 4) % 2), wrap(y + i % 4, N_Y)
        return tx, tx * EIGHTHS + tc * N_Y + ty, tx * 2 + tc, (gx_of(z, tx, tc), ty)

    def mate_from(i):
        tx, tc, ty = wrap(x - i // 8, N_X), flip(core, (i // 4) % 2), wrap(y - i % 4, N_Y)
        return tx, tx * EIGHTHS + tc * N_Y + ty

    def along_z(dz):
        return (gx_of(wrap(z + dz, N_Z), x, core), y)

    barrier = pltpu.get_barrier_semaphore()
    for dz in Z_OFFSETS:
        pl.semaphore_signal(barrier, inc=1, device_id=along_z(dz), device_id_type=MESH)
    for i in range(1, TEAM):
        pl.semaphore_signal(barrier, inc=1, device_id=mate(i)[3], device_id_type=MESH)
    rows_of = [(pos_ref, 0), (pos_ref, 1), (pos_ref, 2), (str_ref, 0), (str_ref, 1), (str_ref, 2)]
    for c in range(N_CORE):
        for b in range(BLK_DEV):
            at = pl.ds(pl.multiple_of(b * BS + (c * N_Y + y) * LANES, LANES), LANES)
            for k, (ref, row) in enumerate(rows_of + [(rad_ref, 0)]):
                own[k // 2, c, b, k % 2 : k % 2 + 1, :] = ref[row : row + 1, at]
            own[3, c, b, 1:2, :] = jnp.zeros((1, LANES), f32)
    pl.semaphore_wait(barrier, TEAM - 1 + len(Z_OFFSETS))

    def home_of(g):
        return grid.at[pl.ds(g * BLK_DEV, BLK_DEV)]

    def row_of(r):
        return grid.at[pl.ds(r * ROW, ROW)]

    sends = []
    for i, (dx, dc) in enumerate(X_OFFSETS):
        tx, tc = wrap(x + dx, N_X), flip(core, dc)
        copy = remote(own.at[tx, tc], home_of(gx), xs.at[i], xr.at[i], (gx_of(z, tx, tc), y))
        copy.start()
        sends.append(copy)
    for b in range(BLK_DEV):
        grid[gx * BLK_DEV + b] = own[x, core, b]
    for i, (dx, dc) in enumerate(X_OFFSETS):
        source = gx_of(z, wrap(x - dx, N_X), flip(core, dc))
        remote(own.at[0, 0], home_of(source), xs.at[i], xr.at[i], other).wait_recv()
    for i, dz in enumerate(Z_OFFSETS):
        copy = remote(row_of(z), row_of(z), gs.at[i], gr.at[i], along_z(dz))
        copy.start()
        sends.append(copy)
    for i, dz in enumerate(Z_OFFSETS):
        row = row_of(wrap(z - dz, N_Z))
        remote(row, row, gs.at[i], gr.at[i], other).wait_recv()

    parts = ((0, 1), (1, EARLY))

    def ask(i, g):
        at = pl.ds(*parts[g])
        return remote(pack.at[i, at], named.at[me, at], ts.at[g, i], tr.at[g, i], mate(i)[3])

    def asked(i, g):
        at = pl.ds(*parts[g])
        member = mate_from(i)[1]
        return remote(pack.at[i, at], named.at[member, at], ts.at[g, i], tr.at[g, i], other)

    for g, (t0, count) in enumerate(parts):

        def send(i, _, g=g, t0=t0, count=count):
            member = mate(i)[1]
            for t in range(t0, t0 + count):
                for k in range(2):
                    block = ids_ref[member * SLOTS + 2 * t + k]
                    pack[i, t, 2 * k : 2 * k + 2, :] = grid[block]
            ask(i, g).start()
            return 0

        lax.fori_loop(1, TEAM, send, 0)
    for t in range(TILES_DEV):
        for k in range(2):
            named[me, t, 2 * k : 2 * k + 2, :] = grid[ids_ref[me * SLOTS + 2 * t + k]]

    lots = ((0, EARLY), (EARLY, 1))

    def give(i, g):
        at = pl.ds(*lots[g])
        _, member, _, to = mate(i)
        return remote(part.at[member, at], team.at[me, at], ps.at[g, i], pr.at[g, i], to)

    def given(i, g):
        at = pl.ds(*lots[g])
        member = mate_from(i)[1]
        return remote(part.at[0, at], team.at[member, at], ps.at[g, i], pr.at[g, i], other)

    def give_all(g):
        def send(i, _):
            @pl.when(mate(i)[0] < 3)
            def _():
                give(i, g).start()

            return 0

        lax.fori_loop(1, TEAM, send, 0)

    def wait_asked(g):
        def wait(i, _):
            asked(i, g).wait_recv()
            return 0

        lax.fori_loop(1, TEAM, wait, 0)

    def one_tile(t, _):
        for g, (t0, _count) in enumerate(parts):
            pl.when(t == t0)(functools.partial(wait_asked, g))

        def rows(k):
            pieces = []
            for e in range(EIGHTHS):
                pairs_of = [named[q * EIGHTHS + e, t, 2 * k : 2 * k + 2, :] for q in range(N_X)]
                pieces.append(jnp.concatenate(pairs_of, 0))
            return jnp.concatenate(pieces, 1)

        v1, s1, v2, s2 = tile_rates(rows(0), rows(1), 128)
        for k, v, st in ((0, v1, s1), (1, v2, s2)):
            full = jnp.concatenate([v, st], 0)
            for q in range(3):
                for e in range(EIGHTHS):
                    piece = full[2 * q : 2 * q + 2, LANES * e : LANES * (e + 1)]
                    part[q * EIGHTHS + e, t, 2 * k : 2 * k + 2, :] = piece
        for g, (t0, count) in enumerate(lots):
            pl.when(t == t0 + count - 1)(functools.partial(give_all, g))
        return 0

    lax.fori_loop(0, TILES_DEV, one_tile, 0)

    @pl.when(active)
    def _():
        team[me] = part[me]
        r = lax.broadcasted_iota(jnp.int32, (8 * N_Z * 8, 1), 0)
        key = ((r // 8) * BLK_DEV + r % 4) * 2 + (r % 8) // 4
        pick[...] = jnp.where(key == keys_ref[...], 1.0, 0.0).astype(bf16)

        def wait(i, _):
            for g in range(2):
                given(i, g).wait_recv()
            return 0

        lax.fori_loop(1, TEAM, wait, 0)
        terms = jnp.concatenate(split3(team[...].reshape(TEAM * TILES_DEV * 4, LANES)), 1)
        sums = lax.dot_general(pick[...], terms, NN, preferred_element_type=f32)
        sums = sums[:, 0:LANES] + (sums[:, LANES : 2 * LANES] + sums[:, 2 * LANES :])
        dense[...] = sums.reshape(N_Z, 8, 8, LANES)
        for i, dz in enumerate(Z_OFFSETS):
            there = dense.at[wrap(z + dz, N_Z)]
            remote(there, zin.at[i], zs.at[i], zr.at[i], along_z(dz)).start()
        for i in range(7):
            remote(dense.at[0], zin.at[i], zs.at[i], zr.at[i], other).wait_recv()
        total = dense[z]
        for i in range(7):
            total = total + zin[i]
        dense[z] = total
        fin[me] = dense[z, x * 2 + core]

        def send(i, _):
            _, _, column, to = mate(i)
            remote(dense.at[z, column], fin.at[me], fs.at[i], fr.at[i], to).start()
            return 0

        lax.fori_loop(1, TEAM, send, 0)

    def settle(i, _):
        for g in range(2):
            ask(i, g).wait_send()

        @pl.when(mate(i)[0] < 3)
        def _():
            for g in range(2):
                give(i, g).wait_send()

        return 0

    lax.fori_loop(1, TEAM, settle, 0)
    for copy in sends:
        copy.wait_send()

    def last(i, _):
        from_x, member = mate_from(i)

        @pl.when(from_x < 3)
        def _():
            remote(dense.at[0, 0], fin.at[member], fs.at[i], fr.at[i], other).wait_recv()

        @pl.when(active)
        def _():
            _, _, column, to = mate(i)
            remote(dense.at[z, column], fin.at[me], fs.at[i], fr.at[i], to).wait_send()

        return 0

    lax.fori_loop(1, TEAM, last, 0)

    @pl.when(active)
    def _():
        for i, dz in enumerate(Z_OFFSETS):
            there = dense.at[wrap(z + dz, N_Z)]
            remote(there, zin.at[i], zs.at[i], zr.at[i], along_z(dz)).wait_send()

    outs = [(vel_out, 0), (vel_out, 1), (vel_out, 2), (str_out, 0), (str_out, 1), (str_out, 2)]
    for q in range(3):
        for e in range(EIGHTHS):
            full = fin[q * EIGHTHS + e]
            for c in range(2):
                ref, row = outs[2 * q + c]
                for b in range(BLK_DEV):
                    at = slice(b * BS + e * LANES, b * BS + (e + 1) * LANES)
                    ref[row : row + 1, at] = full[c * 4 + b : c * 4 + b + 1]


def run(ids, keys, positions, strengths, radii):
    vmem, smem = pl.BlockSpec(memory_space=pltpu.VMEM), pl.BlockSpec(memory_space=pltpu.SMEM)
    dma = pltpu.SemaphoreType.DMA
    out = jax.ShapeDtypeStruct((3, BLK_DEV * BS), f32)
    buffers = [
        (N_X, N_CORE, BLK_DEV, 2, LANES),
        (NB, 2, LANES),
        (TEAM, TILES_DEV, 4, LANES),
        (TEAM, TILES_DEV, 4, LANES),
        (SENDERS, TILES_DEV, 4, LANES),
        (TEAM, TILES_DEV, 4, LANES),
    ]
    late = [(N_Z, 8, 8, LANES), (7, 8, 8, LANES), (SENDERS, 8, LANES)]
    counts = [(7,), (7,), (2, TEAM), (2, TEAM), (7,), (TEAM,)]
    return pl.pallas_call(
        kernel,
        out_shape=(out, out),
        in_specs=[smem, vmem, vmem, vmem, vmem],
        out_specs=(vmem, vmem),
        scratch_shapes=[pltpu.VMEM(b, f32) for b in buffers]
        + [pltpu.VMEM((8 * N_Z * 8, TEAM * TILES_DEV * 4), bf16)]
        + [pltpu.VMEM(b, f32) for b in late]
        + [dma(c) for c in counts for _ in range(2)],
        compiler_params=pltpu.CompilerParams(
            collective_id=0, has_side_effects=True, vmem_limit_bytes=48 * 2**20
        ),
    )(ids, keys, positions, strengths, radii)


def body(positions, strengths, core_radii, tile_pairs, block_home):
    z = lax.axis_index("gx") // (2 * N_X)
    teams = tile_pairs.reshape(N_Z, TEAM * SLOTS)
    logical = lax.dynamic_index_in_dim(teams, z, 0, keepdims=False)
    blocks = jnp.arange(NB, dtype=jnp.int32)
    stored = jnp.sum(jnp.where(logical[:, None] == blocks, block_home, 0), axis=1)
    keys = (stored[:, None] * 2 + jnp.arange(2, dtype=jnp.int32)).reshape(1, -1)
    return run(stored, keys, positions, strengths, core_radii[None, :])


def solution(mesh):
    return jax.shard_map(
        body,
        mesh=mesh,
        in_specs=(P(None, "gx"), P(None, "gx"), P("gx"), P(), P()),
        out_specs=(P(None, "gx"), P(None, "gx")),
        check_vma=False,
    )
```

time: 445 us -> 97.2 us (0.22)
  waiting for transfers between devices: 280 us -> 0 us
  other arithmetic: 134 us -> 0.37 us
  Pallas kernels: 0 us -> 91.6 us
  between operations: 13.9 us -> 0.72 us
  local copies, waits for them, and re-layouts: 13.7 us -> 4.34 us
    reduce_scatter x1 -> x0, waiting for transfers between devices: 144 us -> none  [body(): lax.psum_scatter(totals.reshape(6, -1), 'gx', scatter_dimension=1, tiled=...]
    reduce_sum x17 -> x1, other arithmetic: 128 us -> 0.23 us  [body(): jnp.sum(jnp.where(logical[:, None] == blocks, block_home, 0), axis=1)]
    pallas_call x0 -> x1, Pallas kernels: none -> 91.6 us  [run(): pl.pallas_call(kernel, out_shape=(out, out), in_specs=[smem, vmem, vmem,...]
    all_gather x1 -> x0, waiting for transfers between devices: 86.2 us -> none  [body(): lax.all_gather(resident, 'gx', axis=1, tiled=True).reshape(7, -1, BS)]
    psum x1 -> x0, waiting for transfers between devices: 49.7 us -> none  [body(): rates = lax.psum(share, 'gy')]
  transfers between devices with their start and end apart: 3 -> 0, of which waited for: 3 -> 0; matrix products, arithmetic and copies ran while one was open for 1% -> 0% of each run, Pallas kernels for 0% -> 0%
where the time goes in v3:
time: 97.2 us; the launch traced here: 97 us
  Pallas kernels  91.6 us (94%)
  local copies, waits for them, and re-layouts  4.34 us (4%)
    pallas_call x1, Pallas kernels, run(): pl.pallas_call(kernel, out_shape=(out, out), in_specs=[smem, vmem, vmem,...  91.6 us
    unnamed x11, local copies, waits for them, and re-layouts  3.69 us

profile of v3, /device:TPU:1, one launch (start us, length us, event | category | flops | bytes accessed | tf_op | source)
XLA Modules:
  0.0 97.0 jit_solution(8680133955261211852)
XLA Ops:
  0.6 1.1 %copy.8 = s32[2048,2]{1,0:T(8,128)S(1)} copy(s32[2048,2]{0,1:T(2,128)} %param.8) | data formatting | bytes 32768 | tf_op args[3]
  1.7 0.5 reshape.36
  2.2 0.0 copy-start.3
  2.2 0.7 copy-done.3
  2.9 0.2 select_reduce_fusion.ids_ref
  3.1 0.1 iota_add_fusion
  3.3 0.0 copy-start
  3.3 0.0 copy-start.1
  3.3 0.0 copy-start.2
  3.3 0.2 add.32.keys_ref
  3.5 0.6 copy-done
  4.1 0.0 copy-done.1
  4.2 0.0 copy-done.2
  4.2 91.6 %shard_map.68 = (f32[3,4096]{1,0:T(4,128)S(1)}, f32[3,4096]{1,0:T(4,128)S(1)}) custom-call(s32[512]{0:T(512)S(1)} %select_reduce_fusion.ids_ref, s32[1,1024]{1,0:T(1,128)S(1)} %add.32.keys_ref, f32[3,4096]{1,0:T(4,128)S(1)} %copy-done, f32[3,4096]{1,0:T(4,128)S(1)} %copy-done.1, f32[1,4096]{1,0:T(1,128)S(1)} %bitcast.2), custom_call_target="tpu_custom_call" | custom-call | tf_op jit(solution)/shard_map/pallas_call | solution.py:368
  95.7 0.6 copy.11
  96.4 0.6 copy.12
  (2 shorter events, 0.0 us)
Async XLA Ops:
  2.2 0.7 copy-start.3
  3.3 0.8 copy-start
  3.3 0.9 copy-start.1
  3.3 0.9 copy-start.2

commit v4 on v3

v4 whole, which is shorter than its diff:
```python
import functools

import jax
import jax.numpy as jnp
from jax import lax
from jax.experimental import pallas as pl
from jax.experimental.pallas import tpu as pltpu
from jax.sharding import PartitionSpec as P

BS = 1024
TILES_DEV = 8
BLK_DEV = 4
N_Z, N_X, N_CORE, N_Y = 8, 4, 2, 4
N_J = N_X * N_CORE
TEAM = N_Z * N_Y
SLOTS = 2 * TILES_DEV
NB = 256
ROW = BLK_DEV * N_Z
EARLY = TILES_DEV - 1
LANES = 128
MESH = pl.DeviceIdType.MESH

inv_four_pi = 0.07957747154594767
f32, bf16 = jnp.float32, jnp.bfloat16
NT = (((1,), (1,)), ((), ()))
NN = (((1,), (0,)), ((), ()))


def split3(a):
    hi = a.astype(bf16)
    rest = a - hi.astype(f32)
    mid = rest.astype(bf16)
    lo = (rest - mid.astype(f32)).astype(bf16)
    return hi, mid, lo


def split2(v):
    hi = v.astype(bf16)
    return hi, (v - hi.astype(f32)).astype(bf16)


def cross_rows(a, b):
    a0, a1, a2 = (a[k : k + 1] for k in range(3))
    b0, b1, b2 = (b[k : k + 1] for k in range(3))
    return jnp.concatenate([a1 * b2 - a2 * b1, a2 * b0 - a0 * b2, a0 * b1 - a1 * b0], 0)


def moments(x, w):
    base = jnp.concatenate([w, cross_rows(x, w), jnp.zeros((2, w.shape[1]), f32)], 0)
    parts = [base] + [x[k : k + 1] * base for k in range(3)]
    full = split3(jnp.concatenate(parts, 0))
    return jnp.concatenate([s[:8] for s in full], 0), jnp.concatenate(full, 0)


def gains(x, w, a, s):
    a = a[0:8] + (a[8:16] + a[16:24])
    s = s[0:32] + (s[32:64] + s[64:96])
    along = x[0:1] * w[0:1] + x[1:2] * w[1:2] + x[2:3] * w[2:3]
    t = along * s[0:8] - (w[0:1] * s[8:16] + w[1:2] * s[16:24] + w[2:3] * s[24:32])
    vel = (cross_rows(x, a[0:3]) - a[3:6]) * -inv_four_pi
    turn = cross_rows(x, t[0:3]) - t[3:6]
    stretch = (3.0 * inv_four_pi) * turn - inv_four_pi * cross_rows(w, a[0:3])
    return vel, stretch


def tile_rates(first, second, piece):
    n = first.shape[1]
    total = jnp.sum(first[0:3], axis=1, keepdims=True) + jnp.sum(second[0:3], axis=1, keepdims=True)
    centre = total * (0.5 / n)
    xp, xq = first[0:3] - centre, second[0:3] - centre
    wp, wq = first[3:6], second[3:6]
    sp, sq = 0.5 * first[6:7] * first[6:7], 0.5 * second[6:7] * second[6:7]
    bp, mp = moments(xp, wp)
    bq, mq = moments(xq, wq)
    cols = jnp.transpose(jnp.concatenate([first[0:3], sp, first[4:8]], 0))
    aq = jnp.zeros((24, n), f32)
    hq = jnp.zeros((96, n), f32)
    ap, hp = [], []
    dot = functools.partial(lax.dot_general, preferred_element_type=f32)
    for s in range(0, n, piece):
        cs = cols[s : s + piece]
        r = [cs[:, k : k + 1] - second[k : k + 1] for k in range(3)]
        g = r[0] * r[0] + r[1] * r[1] + r[2] * r[2] + (cs[:, 3:4] + sq)
        q = lax.rsqrt(g)
        q2 = q * q
        f = q2 * q
        h = f * q2
        fh, fl = split2(f)
        hh, hl = split2(h)
        ap.append(dot(fh, bq, NT) + dot(fl, bq, NT))
        hp.append(dot(hh, mq, NT) + dot(hl, mq, NT))
        bps, mps = bp[:, s : s + piece], mp[:, s : s + piece]
        aq = aq + (dot(bps, fh, NN) + dot(bps, fl, NN))
        hq = hq + (dot(mps, hh, NN) + dot(mps, hl, NN))
    ap, hp = jnp.transpose(jnp.concatenate(ap, 0)), jnp.transpose(jnp.concatenate(hp, 0))
    return gains(xp, wp, ap, hp) + gains(xq, wq, aq, hq)


def place():
    gx, y = lax.axis_index("gx"), lax.axis_index("gy")
    return gx // N_J, lax.rem(gx, N_J), y


def wrap(v, n):
    return lax.rem(v + n, n)


J_STEPS = [(2, 0), (2, 1), (1, 0), (3, 0), (1, 1), (3, 1), (0, 1)]
Z_STEPS = [4, 3, 5, 2, 6, 1, 7]


def remote(src, dst, send, recv, device):
    return pltpu.make_async_remote_copy(
        src_ref=src, dst_ref=dst, send_sem=send, recv_sem=recv, device_id=device, device_id_type=MESH
    )


def iota(shape, axis):
    return lax.broadcasted_iota(jnp.int32, shape, axis)


def dot32(a, b):
    return lax.dot_general(a, b, NN, preferred_element_type=f32)


def kernel(
    pairs_ref, home_ref, pairs_vec, home_vec, pos_ref, str_ref, rad_ref, vel_out, str_out,
    mix, own, grid, pack, named, part, team, final_team, dense, jin, fin, pick, final_pick,
    os, orr, gs, gr, ts, tr, ps, pr, js, jr, fs, fr,
):
    z, j, y = place()
    x, core = j // 2, lax.rem(j, 2)
    gx = z * N_J + j
    me = z * N_Y + y
    other = (gx, wrap(y + 1, N_Y))
    active = y < 3

    def mate(i):
        tz, ty = wrap(z + i // N_Y, N_Z), wrap(y + i % N_Y, N_Y)
        return tz, ty, tz * N_Y + ty, (tz * N_J + j, ty)

    def mate_from(i):
        tz, ty = wrap(z - i // N_Y, N_Z), wrap(y - i % N_Y, N_Y)
        return ty, tz * N_Y + ty

    def near(step, way=1):
        dx, dc = step
        return wrap(x + way * dx, N_X) * 2 + lax.rem(core + dc, 2)

    barrier = pltpu.get_barrier_semaphore()
    for i in list(range(1, TEAM)):
        pl.semaphore_signal(barrier, inc=1, device_id=mate(i)[3], device_id_type=MESH)
    for step in J_STEPS:
        to = (z * N_J + near(step), y)
        pl.semaphore_signal(barrier, inc=1, device_id=to, device_id_type=MESH)

    rows_of = [(pos_ref, 0), (pos_ref, 1), (pos_ref, 2), (str_ref, 0), (str_ref, 1), (str_ref, 2)]
    for k, (ref, row) in enumerate(rows_of + [(rad_ref, 0)]):
        mix[k // 2, k % 2 : k % 2 + 1, :] = ref[row : row + 1, :]
    mix[3, 1:2, :] = jnp.zeros((1, BLK_DEV * BS), f32)
    for tz in range(N_Z):
        for b in range(BLK_DEV):
            own[tz, b] = mix[y, :, b * BS + tz * LANES : b * BS + (tz + 1) * LANES]

    def numbers(lanes, row_at):
        chosen = jnp.where(iota((2 * TEAM * TILES_DEV * 4, lanes), 0) == row_at, 1.0, 0.0)
        logical = dot32(pairs_vec[...].astype(f32).astype(bf16), chosen.astype(bf16))
        home = jnp.broadcast_to(home_vec[...], (8, NB)).astype(f32).astype(bf16)
        stored = []
        for k in range(2):
            match = jnp.where(iota((NB, lanes), 0).astype(f32) == logical[k : k + 1], 1.0, 0.0)
            stored.append(dot32(home, match.astype(bf16))[0:1])
        return stored

    r = iota((8 * N_J * N_Z, 1), 0)
    row_key = (((r // 8) * BLK_DEV + r % 4) * 2 + (r % 8) // 4).astype(f32)

    def one_hot(key):
        return jnp.where(row_key == key, 1.0, 0.0).astype(bf16)

    lanes = TEAM * TILES_DEV
    k = iota((1, lanes), 1)
    stored = numbers(lanes, ((k // 32) * N_J + j) * 32 + k % 32)
    for kc in range(4):
        pick[:, lanes * kc : lanes * (kc + 1)] = one_hot(stored[kc // 2] * 2.0 + kc % 2)
    k = iota((1, 4 * TEAM), 1)
    m = k % TEAM
    stored = numbers(4 * TEAM, ((m // N_Y) * N_J + j) * 32 + (m % N_Y) * TILES_DEV + TILES_DEV - 1)
    key = jnp.where(k < 2 * TEAM, stored[0], stored[1]) * 2.0 + ((k // TEAM) % 2).astype(f32)
    final_pick[...] = one_hot(key)
    for m in range(TEAM):
        team[m, TILES_DEV - 1] = jnp.zeros((4, LANES), f32)
    pl.semaphore_wait(barrier, TEAM - 1 + len(J_STEPS))

    def home_of(tj, tz):
        return grid.at[pl.ds(tj * ROW + tz * BLK_DEV, BLK_DEV)]

    def row_of(tj):
        return grid.at[pl.ds(tj * ROW, ROW)]

    sends = []
    for i, dz in enumerate(Z_STEPS):
        tz = wrap(z + dz, N_Z)
        copy = remote(own.at[tz], home_of(j, z), os.at[i], orr.at[i], (tz * N_J + j, y))
        copy.start()
        sends.append(copy)
    for b in range(BLK_DEV):
        grid[j * ROW + z * BLK_DEV + b] = own[z, b]
    for i, dz in enumerate(Z_STEPS):
        there = home_of(j, wrap(z - dz, N_Z))
        remote(own.at[0], there, os.at[i], orr.at[i], other).wait_recv()
    for i, step in enumerate(J_STEPS):
        copy = remote(row_of(j), row_of(j), gs.at[i], gr.at[i], (z * N_J + near(step), y))
        copy.start()
        sends.append(copy)
    for i, step in enumerate(J_STEPS):
        row = row_of(near(step, -1))
        remote(row, row, gs.at[i], gr.at[i], other).wait_recv()

    parts = ((0, 1), (1, EARLY))

    def block_of(tz, ty, t, k):
        row = (tz * N_J + j) * 32 + ty * TILES_DEV + t
        return home_ref[pairs_ref[k * 2 * TEAM * TILES_DEV * 4 + row]]

    def ask(i, g):
        at = pl.ds(*parts[g])
        return remote(pack.at[i, at], named.at[me, at], ts.at[g, i], tr.at[g, i], mate(i)[3])

    def asked(i, g):
        at = pl.ds(*parts[g])
        member = mate_from(i)[1]
        return remote(pack.at[i, at], named.at[member, at], ts.at[g, i], tr.at[g, i], other)

    for g, (t0, count) in enumerate(parts):

        def send(i, _, g=g, t0=t0, count=count):
            tz, ty, _, _ = mate(i)
            for t in range(t0, t0 + count):
                for k in range(2):
                    pack[i, t, 2 * k : 2 * k + 2, :] = grid[block_of(tz, ty, t, k)]
            ask(i, g).start()
            return 0

        lax.fori_loop(1, TEAM, send, 0)
    for t in range(TILES_DEV):
        for k in range(2):
            named[me, t, 2 * k : 2 * k + 2, :] = grid[block_of(z, y, t, k)]

    lots = ((0, EARLY), (EARLY, 1))

    def give(i, g):
        at = pl.ds(*lots[g])
        _, _, member, to = mate(i)
        there = team.at[me, at] if g == 0 else final_team.at[pl.ds(me, 1)]
        return remote(part.at[member, at], there, ps.at[g, i], pr.at[g, i], to)

    def given(i, g):
        at = pl.ds(*lots[g])
        member = mate_from(i)[1]
        here = team.at[member, at] if g == 0 else final_team.at[pl.ds(member, 1)]
        return remote(part.at[0, at], here, ps.at[g, i], pr.at[g, i], other)

    def give_all(g):
        def send(i, _):
            @pl.when(mate(i)[1] < 3)
            def _():
                give(i, g).start()

            return 0

        lax.fori_loop(1, TEAM, send, 0)

    def wait_asked(g):
        def wait(i, _):
            asked(i, g).wait_recv()
            return 0

        lax.fori_loop(1, TEAM, wait, 0)

    def one_tile(t, _):
        for g, (t0, _count) in enumerate(parts):
            pl.when(t == t0)(functools.partial(wait_asked, g))

        def rows(k):
            pieces = []
            for e in range(N_Z):
                pairs_of = [named[e * N_Y + q, t, 2 * k : 2 * k + 2, :] for q in range(N_Y)]
                pieces.append(jnp.concatenate(pairs_of, 0))
            return jnp.concatenate(pieces, 1)

        v1, s1, v2, s2 = tile_rates(rows(0), rows(1), 128)
        for k, v, st in ((0, v1, s1), (1, v2, s2)):
            full = jnp.concatenate([v, st], 0)
            for q in range(3):
                for e in range(N_Z):
                    piece = full[2 * q : 2 * q + 2, LANES * e : LANES * (e + 1)]
                    part[e * N_Y + q, t, 2 * k : 2 * k + 2, :] = piece
        for g, (t0, count) in enumerate(lots):
            pl.when(t == t0 + count - 1)(functools.partial(give_all, g))
        return 0

    lax.fori_loop(0, TILES_DEV, one_tile, 0)

    def by_block(chosen, terms):
        sums = dot32(chosen, jnp.concatenate(split3(terms), 1))
        return sums[:, 0:LANES] + (sums[:, LANES : 2 * LANES] + sums[:, 2 * LANES :])

    @pl.when(active)
    def _():
        team[me, 0:EARLY] = part[me, 0:EARLY]
        final_team[me] = part[me, EARLY]

        def wait(g, i, _):
            given(i, g).wait_recv()
            return 0

        lax.fori_loop(1, TEAM, functools.partial(wait, 0), 0)
        lanes = TEAM * TILES_DEV
        terms = jnp.concatenate([team[:, :, kc, :].reshape(lanes, LANES) for kc in range(4)], 0)
        sums = by_block(pick[...], terms)
        lax.fori_loop(1, TEAM, functools.partial(wait, 1), 0)
        terms = jnp.concatenate([final_team[:, kc, :] for kc in range(4)], 0)
        sums = sums + by_block(final_pick[...], terms)
        dense[...] = sums.reshape(N_J, N_Z, 8, LANES)
        for i, step in enumerate(J_STEPS):
            tj = near(step)
            remote(dense.at[tj], jin.at[i], js.at[i], jr.at[i], (z * N_J + tj, y)).start()
        for i in range(7):
            remote(dense.at[0], jin.at[i], js.at[i], jr.at[i], other).wait_recv()
        total = dense[j]
        for i in range(7):
            total = total + jin[i]
        dense[j] = total
        fin[me] = dense[j, z]

        def send(i, _):
            tz, _, _, to = mate(i)
            remote(dense.at[j, tz], fin.at[me], fs.at[i], fr.at[i], to).start()
            return 0

        lax.fori_loop(1, TEAM, send, 0)

    def settle(i, _):
        for g in range(2):
            ask(i, g).wait_send()

        @pl.when(mate(i)[1] < 3)
        def _():
            for g in range(2):
                give(i, g).wait_send()

        return 0

    lax.fori_loop(1, TEAM, settle, 0)
    for copy in sends:
        copy.wait_send()

    @pl.when(active)
    def _():
        for i, step in enumerate(J_STEPS):
            remote(dense.at[near(step)], jin.at[i], js.at[i], jr.at[i], other).wait_send()

    def last(i, _):
        from_y, member = mate_from(i)

        @pl.when(from_y < 3)
        def _():
            remote(dense.at[0, 0], fin.at[member], fs.at[i], fr.at[i], other).wait_recv()

        @pl.when(active)
        def _():
            tz, _, _, to = mate(i)
            remote(dense.at[j, tz], fin.at[me], fs.at[i], fr.at[i], to).wait_send()

        return 0

    lax.fori_loop(1, TEAM, last, 0)
    outs = [(vel_out, 0), (vel_out, 1), (vel_out, 2), (str_out, 0), (str_out, 1), (str_out, 2)]
    for q in range(3):
        for e in range(N_Z):
            full = fin[e * N_Y + q]
            for c in range(2):
                ref, row = outs[2 * q + c]
                for b in range(BLK_DEV):
                    at = slice(b * BS + e * LANES, b * BS + (e + 1) * LANES)
                    ref[row : row + 1, at] = full[c * 4 + b : c * 4 + b + 1]


def run(pairs, home, positions, strengths, radii):
    vmem, smem = pl.BlockSpec(memory_space=pltpu.VMEM), pl.BlockSpec(memory_space=pltpu.SMEM)
    dma = pltpu.SemaphoreType.DMA
    out = jax.ShapeDtypeStruct((3, BLK_DEV * BS), f32)
    buffers = [
        (N_Y, 2, BLK_DEV * BS),
        (N_Z, BLK_DEV, 2, LANES),
        (NB, 2, LANES),
        (TEAM, TILES_DEV, 4, LANES),
        (TEAM, TILES_DEV, 4, LANES),
        (TEAM, TILES_DEV, 4, LANES),
        (TEAM, TILES_DEV, 4, LANES),
        (TEAM, 4, LANES),
        (N_J, N_Z, 8, LANES),
        (7, N_Z, 8, LANES),
        (TEAM, 8, LANES),
    ]
    chosen = [(8 * N_J * N_Z, 4 * TEAM * TILES_DEV), (8 * N_J * N_Z, 4 * TEAM)]
    counts = [(7,), (7,), (2, TEAM), (2, TEAM), (7,), (TEAM,)]
    return pl.pallas_call(
        kernel,
        out_shape=(out, out),
        in_specs=[smem, smem, vmem, vmem, vmem, vmem, vmem],
        out_specs=(vmem, vmem),
        scratch_shapes=[pltpu.VMEM(b, f32) for b in buffers]
        + [pltpu.VMEM(b, bf16) for b in chosen]
        + [dma(c) for c in counts for _ in range(2)],
        compiler_params=pltpu.CompilerParams(
            collective_id=0, has_side_effects=True, vmem_limit_bytes=48 * 2**20
        ),
    )(pairs.reshape(-1), home, pairs, home[None, :], positions, strengths, radii)


def body(positions, strengths, core_radii, tile_pairs, block_home):
    gx, b = block_home // BLK_DEV, block_home % BLK_DEV
    home = ((gx % N_J) * N_Z + gx // N_J) * BLK_DEV + b
    return run(tile_pairs.T, home, positions, strengths, core_radii[None, :])


def solution(mesh):
    return jax.shard_map(
        body,
        mesh=mesh,
        in_specs=(P(None, "gx"), P(None, "gx"), P("gx"), P(), P()),
        out_specs=(P(None, "gx"), P(None, "gx")),
        check_vma=False,
    )
```

time: 97.2 us -> 98.5 us (1.013)
  Pallas kernels: 91.6 us -> 93.1 us
    pallas_call x1, Pallas kernels: 91.6 us -> 93.1 us  [run(): pl.pallas_call(kernel, out_shape=(out, out), in_specs=[smem, smem, vmem,...]
    unnamed x11 -> x13, local copies, waits for them, and re-layouts: 3.69 us -> 4.39 us
where the time goes in v4:
time: 98.5 us; the launch traced here: 98.2 us
  Pallas kernels  93.1 us (95%)
  local copies, waits for them, and re-layouts  4.39 us (4%)
    pallas_call x1, Pallas kernels, run(): pl.pallas_call(kernel, out_shape=(out, out), in_specs=[smem, smem, vmem,...  93.1 us
    unnamed x13, local copies, waits for them, and re-layouts  4.39 us

profile of v4, /device:TPU:1, one launch (start us, length us, event | category | flops | bytes accessed | tf_op | source)
XLA Modules:
  0.0 98.2 jit_solution(9083807539237934386)
XLA Ops:
  0.6 0.0 copy-start.4
  0.6 0.7 copy-done.4
  1.3 0.0 copy-start
  1.3 0.0 copy-start.3
  1.4 0.8 copy.7
  2.1 0.0 copy-done
  2.1 0.0 copy-done.3
  2.1 0.0 copy-start.1
  2.1 0.8 copy-done.1
  3.0 0.0 copy-start.2
  3.0 0.8 copy-done.2
  3.8 93.1 %shard_map.68 = (f32[3,4096]{1,0:T(4,128)S(1)}, f32[3,4096]{1,0:T(4,128)S(1)}) custom-call(s32[4096]{0:T(1024)S(1)} %bitcast.7, s32[256]{0:T(256)S(1)} %fusion.2.home_ref, s32[2,2048]{1,0:T(2,128)S(1)} %bitcast.6, s32[1,256]{1,0:T(1,128)S(1)} %bitcast.9, f32[3,4096]{1,0:T(4,128)S(1)} %copy-done.1, f32[3,4096]{1,0:T(4,128)S(1)} %copy-done.2, ...), custom_call_target="tpu_custom_call" | custom-call | tf_op jit(solution)/shard_map/pallas_call | solution.py:409
  97.0 0.6 copy.10
  97.6 0.6 copy.11
  (1 shorter events, 0.0 us)
Async XLA Ops:
  0.6 0.7 copy-start.4
  1.3 0.8 copy-start
  1.3 0.8 copy-start.3
  2.1 0.8 copy-start.1
  3.0 0.8 copy-start.2

commit v5 on v4

--- a/solution.py
+++ b/solution.py
@@ -115,6 +115,11 @@
     )
 
 
+def number_of(storage):
+    z, j = lax.shift_right_logical(storage, 5), lax.shift_right_logical(storage, 2) & (N_J - 1)
+    return j * ROW + z * BLK_DEV + (storage & (BLK_DEV - 1))
+
+
 def iota(shape, axis):
     return lax.broadcasted_iota(jnp.int32, shape, axis)
 
@@ -124,9 +129,9 @@
 
 
 def kernel(
-    pairs_ref, home_ref, pairs_vec, home_vec, pos_ref, str_ref, rad_ref, vel_out, str_out,
-    mix, own, grid, pack, named, part, team, final_team, dense, jin, fin, pick, final_pick,
-    os, orr, gs, gr, ts, tr, ps, pr, js, jr, fs, fr,
+    pairs_ref, home_ref, pairs_hbm, home_hbm, pos_hbm, str_hbm, rad_hbm, vel_out, str_out,
+    table, pairs_vec, home_vec, pos_ref, str_ref, rad_ref, mix, own, grid, pack, named, part, team, final_team, dense, jin, fin, pick, final_pick,
+    loads, os, orr, gs, gr, ts, tr, ps, pr, js, jr, fs, fr,
 ):
     z, j, y = place()
     x, core = j // 2, lax.rem(j, 2)
@@ -147,13 +152,26 @@
         dx, dc = step
         return wrap(x + way * dx, N_X) * 2 + lax.rem(core + dc, 2)
 
+    incoming = [(pos_hbm, pos_ref), (str_hbm, str_ref), (rad_hbm, rad_ref)]
+    incoming += [(pairs_hbm, pairs_vec), (home_hbm, home_vec)]
+    incoming = [pltpu.make_async_copy(a, b, loads.at[i]) for i, (a, b) in enumerate(incoming)]
+    for copy in incoming:
+        copy.start()
     barrier = pltpu.get_barrier_semaphore()
-    for i in list(range(1, TEAM)):
-        pl.semaphore_signal(barrier, inc=1, device_id=mate(i)[3], device_id_type=MESH)
-    for step in J_STEPS:
-        to = (z * N_J + near(step), y)
+    greeted = [(wrap(z + dz, N_Z) * N_J + j, y) for dz in Z_STEPS]
+    greeted += [(gx, wrap(y + dy, N_Y)) for dy in (2, 1, 3)]
+    greeted += [(z * N_J + near(step), y) for step in J_STEPS]
+    for to in greeted:
         pl.semaphore_signal(barrier, inc=1, device_id=to, device_id_type=MESH)
 
+
+    def enter(b, _):
+        table[b] = number_of(home_ref[b])
+        return 0
+
+    lax.fori_loop(0, NB, enter, 0, unroll=8)
+    for copy in incoming:
+        copy.wait()
     rows_of = [(pos_ref, 0), (pos_ref, 1), (pos_ref, 2), (str_ref, 0), (str_ref, 1), (str_ref, 2)]
     for k, (ref, row) in enumerate(rows_of + [(rad_ref, 0)]):
         mix[k // 2, k % 2 : k % 2 + 1, :] = ref[row : row + 1, :]
@@ -162,35 +180,7 @@
         for b in range(BLK_DEV):
             own[tz, b] = mix[y, :, b * BS + tz * LANES : b * BS + (tz + 1) * LANES]
 
-    def numbers(lanes, row_at):
-        chosen = jnp.where(iota((2 * TEAM * TILES_DEV * 4, lanes), 0) == row_at, 1.0, 0.0)
-        logical = dot32(pairs_vec[...].astype(f32).astype(bf16), chosen.astype(bf16))
-        home = jnp.broadcast_to(home_vec[...], (8, NB)).astype(f32).astype(bf16)
-        stored = []
-        for k in range(2):
-            match = jnp.where(iota((NB, lanes), 0).astype(f32) == logical[k : k + 1], 1.0, 0.0)
-            stored.append(dot32(home, match.astype(bf16))[0:1])
-        return stored
-
-    r = iota((8 * N_J * N_Z, 1), 0)
-    row_key = (((r // 8) * BLK_DEV + r % 4) * 2 + (r % 8) // 4).astype(f32)
-
-    def one_hot(key):
-        return jnp.where(row_key == key, 1.0, 0.0).astype(bf16)
-
-    lanes = TEAM * TILES_DEV
-    k = iota((1, lanes), 1)
-    stored = numbers(lanes, ((k // 32) * N_J + j) * 32 + k % 32)
-    for kc in range(4):
-        pick[:, lanes * kc : lanes * (kc + 1)] = one_hot(stored[kc // 2] * 2.0 + kc % 2)
-    k = iota((1, 4 * TEAM), 1)
-    m = k % TEAM
-    stored = numbers(4 * TEAM, ((m // N_Y) * N_J + j) * 32 + (m % N_Y) * TILES_DEV + TILES_DEV - 1)
-    key = jnp.where(k < 2 * TEAM, stored[0], stored[1]) * 2.0 + ((k // TEAM) % 2).astype(f32)
-    final_pick[...] = one_hot(key)
-    for m in range(TEAM):
-        team[m, TILES_DEV - 1] = jnp.zeros((4, LANES), f32)
-    pl.semaphore_wait(barrier, TEAM - 1 + len(J_STEPS))
+    pl.semaphore_wait(barrier, len(greeted))
 
     def home_of(tj, tz):
         return grid.at[pl.ds(tj * ROW + tz * BLK_DEV, BLK_DEV)]
@@ -213,15 +203,43 @@
         copy = remote(row_of(j), row_of(j), gs.at[i], gr.at[i], (z * N_J + near(step), y))
         copy.start()
         sends.append(copy)
+    def numbers(lanes, row_at):
+        chosen = jnp.where(iota((2 * TEAM * TILES_DEV * 4, lanes), 0) == row_at, 1.0, 0.0)
+        logical = dot32(pairs_vec[...].astype(f32).astype(bf16), chosen.astype(bf16))
+        home = jnp.broadcast_to(number_of(home_vec[...]), (8, NB)).astype(f32).astype(bf16)
+        stored = []
+        for k in range(2):
+            match = jnp.where(iota((NB, lanes), 0).astype(f32) == logical[k : k + 1], 1.0, 0.0)
+            stored.append(dot32(home, match.astype(bf16))[0:1])
+        return stored
+
+    r = iota((8 * N_J * N_Z, 1), 0)
+    row_key = (((r // 8) * BLK_DEV + r % 4) * 2 + (r % 8) // 4).astype(f32)
+
+    def one_hot(key):
+        return jnp.where(row_key == key, 1.0, 0.0).astype(bf16)
+
+    lanes = TEAM * TILES_DEV
+    k = iota((1, lanes), 1)
+    stored = numbers(lanes, ((k // 32) * N_J + j) * 32 + k % 32)
+    for kc in range(4):
+        pick[:, lanes * kc : lanes * (kc + 1)] = one_hot(stored[kc // 2] * 2.0 + kc % 2)
+    k = iota((1, 4 * TEAM), 1)
+    m = k % TEAM
+    stored = numbers(4 * TEAM, ((m // N_Y) * N_J + j) * 32 + (m % N_Y) * TILES_DEV + TILES_DEV - 1)
+    key = jnp.where(k < 2 * TEAM, stored[0], stored[1]) * 2.0 + ((k // TEAM) % 2).astype(f32)
+    final_pick[...] = one_hot(key)
+    for m in range(TEAM):
+        team[m, TILES_DEV - 1] = jnp.zeros((4, LANES), f32)
     for i, step in enumerate(J_STEPS):
         row = row_of(near(step, -1))
         remote(row, row, gs.at[i], gr.at[i], other).wait_recv()
 
-    parts = ((0, 1), (1, EARLY))
+    parts = ((0, 1), (1, 2), (3, TILES_DEV - 3))
 
     def block_of(tz, ty, t, k):
         row = (tz * N_J + j) * 32 + ty * TILES_DEV + t
-        return home_ref[pairs_ref[k * 2 * TEAM * TILES_DEV * 4 + row]]
+        return table[pairs_ref[k, row]]
 
     def ask(i, g):
         at = pl.ds(*parts[g])
@@ -242,23 +260,27 @@
             ask(i, g).start()
             return 0
 
-        lax.fori_loop(1, TEAM, send, 0)
+        if g == 0:
+            for i in range(1, TEAM):
+                send(i, 0)
+        else:
+            lax.fori_loop(1, TEAM, send, 0)
     for t in range(TILES_DEV):
         for k in range(2):
             named[me, t, 2 * k : 2 * k + 2, :] = grid[block_of(z, y, t, k)]
 
-    lots = ((0, EARLY), (EARLY, 1))
+    lots = ((0, 4), (4, EARLY - 4), (EARLY, 1))
 
     def give(i, g):
         at = pl.ds(*lots[g])
         _, _, member, to = mate(i)
-        there = team.at[me, at] if g == 0 else final_team.at[pl.ds(me, 1)]
+        there = team.at[me, at] if g < 2 else final_team.at[pl.ds(me, 1)]
         return remote(part.at[member, at], there, ps.at[g, i], pr.at[g, i], to)
 
     def given(i, g):
         at = pl.ds(*lots[g])
         member = mate_from(i)[1]
-        here = team.at[member, at] if g == 0 else final_team.at[pl.ds(member, 1)]
+        here = team.at[member, at] if g < 2 else final_team.at[pl.ds(member, 1)]
         return remote(part.at[0, at], here, ps.at[g, i], pr.at[g, i], other)
 
     def give_all(g):
@@ -269,7 +291,11 @@
 
             return 0
 
-        lax.fori_loop(1, TEAM, send, 0)
+        if g == 2:
+            for i in range(1, TEAM):
+                send(i, 0)
+        else:
+            lax.fori_loop(1, TEAM, send, 0)
 
     def wait_asked(g):
         def wait(i, _):
@@ -316,10 +342,11 @@
             return 0
 
         lax.fori_loop(1, TEAM, functools.partial(wait, 0), 0)
+        lax.fori_loop(1, TEAM, functools.partial(wait, 1), 0)
         lanes = TEAM * TILES_DEV
         terms = jnp.concatenate([team[:, :, kc, :].reshape(lanes, LANES) for kc in range(4)], 0)
         sums = by_block(pick[...], terms)
-        lax.fori_loop(1, TEAM, functools.partial(wait, 1), 0)
+        lax.fori_loop(1, TEAM, functools.partial(wait, 2), 0)
         terms = jnp.concatenate([final_team[:, kc, :] for kc in range(4)], 0)
         sums = sums + by_block(final_pick[...], terms)
         dense[...] = sums.reshape(N_J, N_Z, 8, LANES)
@@ -334,20 +361,17 @@
         dense[j] = total
         fin[me] = dense[j, z]
 
-        def send(i, _):
+        for i in range(1, TEAM):
             tz, _, _, to = mate(i)
             remote(dense.at[j, tz], fin.at[me], fs.at[i], fr.at[i], to).start()
-            return 0
-
-        lax.fori_loop(1, TEAM, send, 0)
 
     def settle(i, _):
-        for g in range(2):
+        for g in range(3):
             ask(i, g).wait_send()
 
         @pl.when(mate(i)[1] < 3)
         def _():
-            for g in range(2):
+            for g in range(3):
                 give(i, g).wait_send()
 
         return 0
@@ -391,7 +415,12 @@
     vmem, smem = pl.BlockSpec(memory_space=pltpu.VMEM), pl.BlockSpec(memory_space=pltpu.SMEM)
     dma = pltpu.SemaphoreType.DMA
     out = jax.ShapeDtypeStruct((3, BLK_DEV * BS), f32)
+    n = BLK_DEV * BS
+    words = [(2, 2 * TEAM * TILES_DEV * 4), (1, NB)]
     buffers = [
+        (3, n),
+        (3, n),
+        (1, n),
         (N_Y, 2, BLK_DEV * BS),
         (N_Z, BLK_DEV, 2, LANES),
         (NB, 2, LANES),
@@ -405,25 +434,26 @@
         (TEAM, 8, LANES),
     ]
     chosen = [(8 * N_J * N_Z, 4 * TEAM * TILES_DEV), (8 * N_J * N_Z, 4 * TEAM)]
-    counts = [(7,), (7,), (2, TEAM), (2, TEAM), (7,), (TEAM,)]
+    counts = [(7,), (7,), (3, TEAM), (3, TEAM), (7,), (TEAM,)]
     return pl.pallas_call(
         kernel,
         out_shape=(out, out),
-        in_specs=[smem, smem, vmem, vmem, vmem, vmem, vmem],
+        in_specs=[smem, smem] + [pl.BlockSpec(memory_space=pl.ANY)] * 5,
         out_specs=(vmem, vmem),
-        scratch_shapes=[pltpu.VMEM(b, f32) for b in buffers]
+        scratch_shapes=[pltpu.SMEM((NB,), jnp.int32)]
+        + [pltpu.VMEM(b, jnp.int32) for b in words]
+        + [pltpu.VMEM(b, f32) for b in buffers]
         + [pltpu.VMEM(b, bf16) for b in chosen]
+        + [dma((5,))]
         + [dma(c) for c in counts for _ in range(2)],
         compiler_params=pltpu.CompilerParams(
-            collective_id=0, has_side_effects=True, vmem_limit_bytes=48 * 2**20
+            collective_id=0, has_side_effects=True, vmem_limit_bytes=63 * 2**20
         ),
-    )(pairs.reshape(-1), home, pairs, home[None, :], positions, strengths, radii)
+    )(pairs, home, pairs, home[None, :], positions, strengths, radii)
 
 
 def body(positions, strengths, core_radii, tile_pairs, block_home):
-    gx, b = block_home // BLK_DEV, block_home % BLK_DEV
-    home = ((gx % N_J) * N_Z + gx // N_J) * BLK_DEV + b
-    return run(tile_pairs.T, home, positions, strengths, core_radii[None, :])
+    return run(tile_pairs.T, block_home, positions, strengths, core_radii[None, :])
 
 
 def solution(mesh):

time: 98.5 us -> 92.5 us (0.939)
  Pallas kernels: 93.1 us -> 89.5 us
  local copies, waits for them, and re-layouts: 4.39 us -> 2.15 us
    pallas_call x1, Pallas kernels: 93.1 us -> 89.5 us  [run(): pl.pallas_call(kernel, out_shape=(out, out), in_specs=[smem, smem] + [pl....]
    unnamed x13 -> x4, local copies, waits for them, and re-layouts: 4.39 us -> 2.15 us
where the time goes in v5:
time: 92.5 us; the launch traced here: 92.3 us
  Pallas kernels  89.5 us (97%)
  local copies, waits for them, and re-layouts  2.15 us (2%)
    pallas_call x1, Pallas kernels, run(): pl.pallas_call(kernel, out_shape=(out, out), in_specs=[smem, smem] + [pl....  89.5 us
    unnamed x4, local copies, waits for them, and re-layouts  2.15 us

profile of v5, /device:TPU:1, one launch (start us, length us, event | category | flops | bytes accessed | tf_op | source)
XLA Modules:
  0.0 92.3 jit_solution(14476324877177203198)
XLA Ops:
  0.6 89.5 %shard_map.68 = (f32[3,4096]{1,0:T(4,128)}, f32[3,4096]{1,0:T(4,128)}) custom-call(s32[2,2048]{1,0:T(2,128)} %bitcast.3, s32[256]{0:T(256)} %home_ref.1, s32[2,2048]{1,0:T(2,128)} %bitcast.4, s32[1,256]{1,0:T(1,128)} %bitcast.6, f32[3,4096]{1,0:T(4,128)} %pos_hbm.1, f32[3,4096]{1,0:T(4,128)} %str_hbm.1, f32[1,4096]{1,0:T(1,128)} %bitcast.5), custom_call_target="tpu_custom_call" | custom-call | tf_op jit(solution)/shard_map/pallas_call | solution.py:438
  90.1 0.0 copy-start
  90.1 1.5 %copy.9 = f32[3,4096]{1,0:T(4,128)} copy(f32[3,4096]{1,0:T(4,128)} %get-tuple-element.4) | data formatting | bytes 98304
  91.6 0.0 copy-done
  91.6 0.6 copy.10
Async XLA Ops:
  90.1 1.5 %copy-start = (f32[3,4096]{1,0:T(4,128)S(1)}, f32[3,4096]{1,0:T(4,128)}, u32[]{:S(2)}) copy-start(f32[3,4096]{1,0:T(4,128)} %get-tuple-element.5) | copy-start | bytes 147460

commit v6 on v5

--- a/solution.py
+++ b/solution.py
@@ -16,7 +16,8 @@
 SLOTS = 2 * TILES_DEV
 NB = 256
 ROW = BLK_DEV * N_Z
-EARLY = TILES_DEV - 1
+EARLY = TILES_DEV - 2
+LATE = TILES_DEV - EARLY
 LANES = 128
 MESH = pl.DeviceIdType.MESH
 
@@ -87,11 +88,14 @@
         h = f * q2
         fh, fl = split2(f)
         hh, hl = split2(h)
-        ap.append(dot(fh, bq, NT) + dot(fl, bq, NT))
-        hp.append(dot(hh, mq, NT) + dot(hl, mq, NT))
+        f2, h2 = jnp.concatenate([fh, fl], 0), jnp.concatenate([hh, hl], 0)
+        both = dot(f2, bq, NT)
+        ap.append(both[:piece] + both[piece:])
+        both = dot(h2, mq, NT)
+        hp.append(both[:piece] + both[piece:])
         bps, mps = bp[:, s : s + piece], mp[:, s : s + piece]
-        aq = aq + (dot(bps, fh, NN) + dot(bps, fl, NN))
-        hq = hq + (dot(mps, hh, NN) + dot(mps, hl, NN))
+        aq = aq + dot(jnp.concatenate([bps, bps], 1), f2, NN)
+        hq = hq + dot(jnp.concatenate([mps, mps], 1), h2, NN)
     ap, hp = jnp.transpose(jnp.concatenate(ap, 0)), jnp.transpose(jnp.concatenate(hp, 0))
     return gains(xp, wp, ap, hp) + gains(xq, wq, aq, hq)
 
@@ -224,18 +228,19 @@
     stored = numbers(lanes, ((k // 32) * N_J + j) * 32 + k % 32)
     for kc in range(4):
         pick[:, lanes * kc : lanes * (kc + 1)] = one_hot(stored[kc // 2] * 2.0 + kc % 2)
-    k = iota((1, 4 * TEAM), 1)
-    m = k % TEAM
-    stored = numbers(4 * TEAM, ((m // N_Y) * N_J + j) * 32 + (m % N_Y) * TILES_DEV + TILES_DEV - 1)
-    key = jnp.where(k < 2 * TEAM, stored[0], stored[1]) * 2.0 + ((k // TEAM) % 2).astype(f32)
+    late = TEAM * LATE
+    k = iota((1, 4 * late), 1)
+    m, t = (k % late) // LATE, EARLY + k % LATE
+    stored = numbers(4 * late, ((m // N_Y) * N_J + j) * 32 + (m % N_Y) * TILES_DEV + t)
+    key = jnp.where(k < 2 * late, stored[0], stored[1]) * 2.0 + ((k // late) % 2).astype(f32)
     final_pick[...] = one_hot(key)
     for m in range(TEAM):
-        team[m, TILES_DEV - 1] = jnp.zeros((4, LANES), f32)
+        team[m, EARLY:] = jnp.zeros((LATE, 4, LANES), f32)
     for i, step in enumerate(J_STEPS):
         row = row_of(near(step, -1))
         remote(row, row, gs.at[i], gr.at[i], other).wait_recv()
 
-    parts = ((0, 1), (1, 2), (3, TILES_DEV - 3))
+    parts = ((0, 2), (2, 2), (4, TILES_DEV - 4))
 
     def block_of(tz, ty, t, k):
         row = (tz * N_J + j) * 32 + ty * TILES_DEV + t
@@ -269,18 +274,18 @@
         for k in range(2):
             named[me, t, 2 * k : 2 * k + 2, :] = grid[block_of(z, y, t, k)]
 
-    lots = ((0, 4), (4, EARLY - 4), (EARLY, 1))
+    lots = ((0, 4), (4, EARLY - 4), (EARLY, LATE))
 
     def give(i, g):
         at = pl.ds(*lots[g])
         _, _, member, to = mate(i)
-        there = team.at[me, at] if g < 2 else final_team.at[pl.ds(me, 1)]
+        there = team.at[me, at] if g < 2 else final_team.at[me]
         return remote(part.at[member, at], there, ps.at[g, i], pr.at[g, i], to)
 
     def given(i, g):
         at = pl.ds(*lots[g])
         member = mate_from(i)[1]
-        here = team.at[member, at] if g < 2 else final_team.at[pl.ds(member, 1)]
+        here = team.at[member, at] if g < 2 else final_team.at[member]
         return remote(part.at[0, at], here, ps.at[g, i], pr.at[g, i], other)
 
     def give_all(g):
@@ -292,8 +297,12 @@
             return 0
 
         if g == 2:
-            for i in range(1, TEAM):
-                send(i, 0)
+            for dy in range(N_Y):
+
+                @pl.when(wrap(y + dy, N_Y) < 3)
+                def _(dy=dy):
+                    for i in range(dy if dy else N_Y, TEAM, N_Y):
+                        give(i, g).start()
         else:
             lax.fori_loop(1, TEAM, send, 0)
 
@@ -304,29 +313,32 @@
 
         lax.fori_loop(1, TEAM, wait, 0)
 
-    def one_tile(t, _):
+    def two_tiles(pair, _):
+        t = 2 * pair
         for g, (t0, _count) in enumerate(parts):
             pl.when(t == t0)(functools.partial(wait_asked, g))
 
-        def rows(k):
+        def rows(t, k):
             pieces = []
             for e in range(N_Z):
                 pairs_of = [named[e * N_Y + q, t, 2 * k : 2 * k + 2, :] for q in range(N_Y)]
                 pieces.append(jnp.concatenate(pairs_of, 0))
             return jnp.concatenate(pieces, 1)
 
-        v1, s1, v2, s2 = tile_rates(rows(0), rows(1), 128)
-        for k, v, st in ((0, v1, s1), (1, v2, s2)):
-            full = jnp.concatenate([v, st], 0)
-            for q in range(3):
-                for e in range(N_Z):
-                    piece = full[2 * q : 2 * q + 2, LANES * e : LANES * (e + 1)]
-                    part[e * N_Y + q, t, 2 * k : 2 * k + 2, :] = piece
+        rates = [tile_rates(rows(t + u, 0), rows(t + u, 1), 128) for u in range(2)]
+        for u in range(2):
+            v1, s1, v2, s2 = rates[u]
+            for k, v, st in ((0, v1, s1), (1, v2, s2)):
+                full = jnp.concatenate([v, st], 0)
+                for q in range(3):
+                    for e in range(N_Z):
+                        piece = full[2 * q : 2 * q + 2, LANES * e : LANES * (e + 1)]
+                        part[e * N_Y + q, t + u, 2 * k : 2 * k + 2, :] = piece
         for g, (t0, count) in enumerate(lots):
-            pl.when(t == t0 + count - 1)(functools.partial(give_all, g))
+            pl.when(t + 2 == t0 + count)(functools.partial(give_all, g))
         return 0
 
-    lax.fori_loop(0, TILES_DEV, one_tile, 0)
+    lax.fori_loop(0, TILES_DEV // 2, two_tiles, 0)
 
     def by_block(chosen, terms):
         sums = dot32(chosen, jnp.concatenate(split3(terms), 1))
@@ -335,7 +347,7 @@
     @pl.when(active)
     def _():
         team[me, 0:EARLY] = part[me, 0:EARLY]
-        final_team[me] = part[me, EARLY]
+        final_team[me] = part[me, EARLY:]
 
         def wait(g, i, _):
             given(i, g).wait_recv()
@@ -347,7 +359,8 @@
         terms = jnp.concatenate([team[:, :, kc, :].reshape(lanes, LANES) for kc in range(4)], 0)
         sums = by_block(pick[...], terms)
         lax.fori_loop(1, TEAM, functools.partial(wait, 2), 0)
-        terms = jnp.concatenate([final_team[:, kc, :] for kc in range(4)], 0)
+        terms = [final_team[:, :, kc, :].reshape(TEAM * LATE, LANES) for kc in range(4)]
+        terms = jnp.concatenate(terms, 0)
         sums = sums + by_block(final_pick[...], terms)
         dense[...] = sums.reshape(N_J, N_Z, 8, LANES)
         for i, step in enumerate(J_STEPS):
@@ -428,12 +441,12 @@
         (TEAM, TILES_DEV, 4, LANES),
         (TEAM, TILES_DEV, 4, LANES),
         (TEAM, TILES_DEV, 4, LANES),
-        (TEAM, 4, LANES),
+        (TEAM, LATE, 4, LANES),
         (N_J, N_Z, 8, LANES),
         (7, N_Z, 8, LANES),
         (TEAM, 8, LANES),
     ]
-    chosen = [(8 * N_J * N_Z, 4 * TEAM * TILES_DEV), (8 * N_J * N_Z, 4 * TEAM)]
+    chosen = [(8 * N_J * N_Z, 4 * TEAM * TILES_DEV), (8 * N_J * N_Z, 4 * TEAM * LATE)]
     counts = [(7,), (7,), (3, TEAM), (3, TEAM), (7,), (TEAM,)]
     return pl.pallas_call(
         kernel,

time: 92.5 us -> 90.8 us (0.982)
  Pallas kernels: 89.5 us -> 87.8 us
    pallas_call x1, Pallas kernels: 89.5 us -> 87.8 us  [run(): pl.pallas_call(kernel, out_shape=(out, out), in_specs=[smem, smem] + [pl....]
where the time goes in v6:
time: 90.8 us; the launch traced here: 90.6 us
  Pallas kernels  87.8 us (97%)
  local copies, waits for them, and re-layouts  2.15 us (2%)
    pallas_call x1, Pallas kernels, run(): pl.pallas_call(kernel, out_shape=(out, out), in_specs=[smem, smem] + [pl....  87.8 us
    unnamed x4, local copies, waits for them, and re-layouts  2.15 us

profile of v6, /device:TPU:1, one launch (start us, length us, event | category | flops | bytes accessed | tf_op | source)
XLA Modules:
  0.0 90.6 jit_solution(11963933147652565035)
XLA Ops:
  0.6 87.8 %shard_map.68 = (f32[3,4096]{1,0:T(4,128)}, f32[3,4096]{1,0:T(4,128)}) custom-call(s32[2,2048]{1,0:T(2,128)} %bitcast.3, s32[256]{0:T(256)} %home_ref.1, s32[2,2048]{1,0:T(2,128)} %bitcast.4, s32[1,256]{1,0:T(1,128)} %bitcast.6, f32[3,4096]{1,0:T(4,128)} %pos_hbm.1, f32[3,4096]{1,0:T(4,128)} %str_hbm.1, f32[1,4096]{1,0:T(1,128)} %bitcast.5), custom_call_target="tpu_custom_call" | custom-call | tf_op jit(solution)/shard_map/pallas_call | solution.py:451
  88.4 0.0 copy-start
  88.4 1.5 %copy.9 = f32[3,4096]{1,0:T(4,128)} copy(f32[3,4096]{1,0:T(4,128)} %get-tuple-element.4) | data formatting | bytes 98304
  89.9 0.0 copy-done
  89.9 0.6 copy.10
Async XLA Ops:
  88.4 1.5 %copy-start = (f32[3,4096]{1,0:T(4,128)S(1)}, f32[3,4096]{1,0:T(4,128)}, u32[]{:S(2)}) copy-start(f32[3,4096]{1,0:T(4,128)} %get-tuple-element.5) | copy-start | bytes 147460

commit v7 on v6

--- a/solution.py
+++ b/solution.py
@@ -169,11 +169,6 @@
         pl.semaphore_signal(barrier, inc=1, device_id=to, device_id_type=MESH)
 
 
-    def enter(b, _):
-        table[b] = number_of(home_ref[b])
-        return 0
-
-    lax.fori_loop(0, NB, enter, 0, unroll=8)
     for copy in incoming:
         copy.wait()
     rows_of = [(pos_ref, 0), (pos_ref, 1), (pos_ref, 2), (str_ref, 0), (str_ref, 1), (str_ref, 2)]
@@ -207,6 +202,12 @@
         copy = remote(row_of(j), row_of(j), gs.at[i], gr.at[i], (z * N_J + near(step), y))
         copy.start()
         sends.append(copy)
+    def enter(b, _):
+        table[b] = number_of(home_ref[b])
+        return 0
+
+    lax.fori_loop(0, NB, enter, 0, unroll=8)
+
     def numbers(lanes, row_at):
         chosen = jnp.where(iota((2 * TEAM * TILES_DEV * 4, lanes), 0) == row_at, 1.0, 0.0)
         logical = dot32(pairs_vec[...].astype(f32).astype(bf16), chosen.astype(bf16))
@@ -257,19 +258,15 @@
 
     for g, (t0, count) in enumerate(parts):
 
-        def send(i, _, g=g, t0=t0, count=count):
+        def send(i, g=g, t0=t0, count=count):
             tz, ty, _, _ = mate(i)
             for t in range(t0, t0 + count):
                 for k in range(2):
                     pack[i, t, 2 * k : 2 * k + 2, :] = grid[block_of(tz, ty, t, k)]
             ask(i, g).start()
-            return 0
-
-        if g == 0:
-            for i in range(1, TEAM):
-                send(i, 0)
-        else:
-            lax.fori_loop(1, TEAM, send, 0)
+
+        for i in range(1, TEAM):
+            send(i)
     for t in range(TILES_DEV):
         for k in range(2):
             named[me, t, 2 * k : 2 * k + 2, :] = grid[block_of(z, y, t, k)]
@@ -289,22 +286,12 @@
         return remote(part.at[0, at], here, ps.at[g, i], pr.at[g, i], other)
 
     def give_all(g):
-        def send(i, _):
-            @pl.when(mate(i)[1] < 3)
-            def _():
-                give(i, g).start()
-
-            return 0
-
-        if g == 2:
-            for dy in range(N_Y):
-
-                @pl.when(wrap(y + dy, N_Y) < 3)
-                def _(dy=dy):
-                    for i in range(dy if dy else N_Y, TEAM, N_Y):
-                        give(i, g).start()
-        else:
-            lax.fori_loop(1, TEAM, send, 0)
+        for dy in range(N_Y):
+
+            @pl.when(wrap(y + dy, N_Y) < 3)
+            def _(dy=dy):
+                for i in range(dy if dy else N_Y, TEAM, N_Y):
+                    give(i, g).start()
 
     def wait_asked(g):
         def wait(i, _):

time: 90.8 us -> 89.8 us (0.989)
  Pallas kernels: 87.8 us -> 86.7 us
    pallas_call x1, Pallas kernels: 87.8 us -> 86.7 us  [run(): pl.pallas_call(kernel, out_shape=(out, out), in_specs=[smem, smem] + [pl....]
where the time goes in v7:
time: 89.8 us; the launch traced here: 89.5 us
  Pallas kernels  86.7 us (97%)
  local copies, waits for them, and re-layouts  2.15 us (2%)
    pallas_call x1, Pallas kernels, run(): pl.pallas_call(kernel, out_shape=(out, out), in_specs=[smem, smem] + [pl....  86.7 us
    unnamed x4, local copies, waits for them, and re-layouts  2.15 us

profile of v7, /device:TPU:1, one launch (start us, length us, event | category | flops | bytes accessed | tf_op | source)
XLA Modules:
  0.0 89.5 jit_solution(15844326364291355747)
XLA Ops:
  0.6 86.7 %shard_map.68 = (f32[3,4096]{1,0:T(4,128)}, f32[3,4096]{1,0:T(4,128)}) custom-call(s32[2,2048]{1,0:T(2,128)} %bitcast.3, s32[256]{0:T(256)} %home_ref.1, s32[2,2048]{1,0:T(2,128)} %bitcast.4, s32[1,256]{1,0:T(1,128)} %bitcast.6, f32[3,4096]{1,0:T(4,128)} %pos_hbm.1, f32[3,4096]{1,0:T(4,128)} %str_hbm.1, f32[1,4096]{1,0:T(1,128)} %bitcast.5), custom_call_target="tpu_custom_call" | custom-call | tf_op jit(solution)/shard_map/pallas_call | solution.py:438
  87.4 0.0 copy-start
  87.4 1.5 %copy.9 = f32[3,4096]{1,0:T(4,128)} copy(f32[3,4096]{1,0:T(4,128)} %get-tuple-element.4) | data formatting | bytes 98304
  88.9 0.0 copy-done
  88.9 0.6 copy.10
Async XLA Ops:
  87.4 1.5 %copy-start = (f32[3,4096]{1,0:T(4,128)S(1)}, f32[3,4096]{1,0:T(4,128)}, u32[]{:S(2)}) copy-start(f32[3,4096]{1,0:T(4,128)} %get-tuple-element.5) | copy-start | bytes 147460

commit v8 on v7

--- a/solution.py
+++ b/solution.py
@@ -111,6 +111,7 @@
 
 J_STEPS = [(2, 0), (2, 1), (1, 0), (3, 0), (1, 1), (3, 1), (0, 1)]
 Z_STEPS = [4, 3, 5, 2, 6, 1, 7]
+MATES = [dz * N_Y + dy for dz in Z_STEPS + [0] for dy in (2, 1, 3, 0) if dz or dy]
 
 
 def remote(src, dst, send, recv, device):
@@ -265,7 +266,7 @@
                     pack[i, t, 2 * k : 2 * k + 2, :] = grid[block_of(tz, ty, t, k)]
             ask(i, g).start()
 
-        for i in range(1, TEAM):
+        for i in MATES:
             send(i)
     for t in range(TILES_DEV):
         for k in range(2):
@@ -286,12 +287,13 @@
         return remote(part.at[0, at], here, ps.at[g, i], pr.at[g, i], other)
 
     def give_all(g):
-        for dy in range(N_Y):
+        for dy in (2, 1, 3, 0):
 
             @pl.when(wrap(y + dy, N_Y) < 3)
             def _(dy=dy):
-                for i in range(dy if dy else N_Y, TEAM, N_Y):
-                    give(i, g).start()
+                for i in MATES:
+                    if i % N_Y == dy:
+                        give(i, g).start()
 
     def wait_asked(g):
         def wait(i, _):
@@ -361,7 +363,7 @@
         dense[j] = total
         fin[me] = dense[j, z]
 
-        for i in range(1, TEAM):
+        for i in MATES:
             tz, _, _, to = mate(i)
             remote(dense.at[j, tz], fin.at[me], fs.at[i], fr.at[i], to).start()
 

time: 89.8 us -> 88.4 us (0.984)
  Pallas kernels: 86.7 us -> 85.3 us
    pallas_call x1, Pallas kernels: 86.7 us -> 85.3 us  [run(): pl.pallas_call(kernel, out_shape=(out, out), in_specs=[smem, smem] + [pl....]
where the time goes in v8:
time: 88.4 us; the launch traced here: 88.1 us
  Pallas kernels  85.3 us (96%)
  local copies, waits for them, and re-layouts  2.15 us (2%)
    pallas_call x1, Pallas kernels, run(): pl.pallas_call(kernel, out_shape=(out, out), in_specs=[smem, smem] + [pl....  85.3 us
    unnamed x4, local copies, waits for them, and re-layouts  2.15 us

profile of v8, /device:TPU:1, one launch (start us, length us, event | category | flops | bytes accessed | tf_op | source)
XLA Modules:
  0.0 88.1 jit_solution(6898213337627092087)
XLA Ops:
  0.6 85.3 %shard_map.68 = (f32[3,4096]{1,0:T(4,128)}, f32[3,4096]{1,0:T(4,128)}) custom-call(s32[2,2048]{1,0:T(2,128)} %bitcast.3, s32[256]{0:T(256)} %home_ref.1, s32[2,2048]{1,0:T(2,128)} %bitcast.4, s32[1,256]{1,0:T(1,128)} %bitcast.6, f32[3,4096]{1,0:T(4,128)} %pos_hbm.1, f32[3,4096]{1,0:T(4,128)} %str_hbm.1, f32[1,4096]{1,0:T(1,128)} %bitcast.5), custom_call_target="tpu_custom_call" | custom-call | tf_op jit(solution)/shard_map/pallas_call | solution.py:440
  86.0 0.0 copy-start
  86.0 1.5 %copy.9 = f32[3,4096]{1,0:T(4,128)} copy(f32[3,4096]{1,0:T(4,128)} %get-tuple-element.4) | data formatting | bytes 98304
  87.5 0.0 copy-done
  87.5 0.6 copy.10
Async XLA Ops:
  86.0 1.5 %copy-start = (f32[3,4096]{1,0:T(4,128)S(1)}, f32[3,4096]{1,0:T(4,128)}, u32[]{:S(2)}) copy-start(f32[3,4096]{1,0:T(4,128)} %get-tuple-element.5) | copy-start | bytes 147460

commit v9 on v8

--- a/solution.py
+++ b/solution.py
@@ -259,15 +259,17 @@
 
     for g, (t0, count) in enumerate(parts):
 
-        def send(i, g=g, t0=t0, count=count):
+        def fill(i, t0=t0, count=count):
             tz, ty, _, _ = mate(i)
             for t in range(t0, t0 + count):
                 for k in range(2):
                     pack[i, t, 2 * k : 2 * k + 2, :] = grid[block_of(tz, ty, t, k)]
-            ask(i, g).start()
-
-        for i in MATES:
-            send(i)
+
+        for first in range(0, len(MATES), 8):
+            for i in MATES[first : first + 8]:
+                fill(i)
+            for i in MATES[first : first + 8]:
+                ask(i, g).start()
     for t in range(TILES_DEV):
         for k in range(2):
             named[me, t, 2 * k : 2 * k + 2, :] = grid[block_of(z, y, t, k)]

time: 88.4 us -> 88.4 us (level)
  no operation moved by 1% of the time
where the time goes in v9:
time: 88.4 us; the launch traced here: 88.1 us
  Pallas kernels  85.3 us (96%)
  local copies, waits for them, and re-layouts  2.15 us (2%)
    pallas_call x1, Pallas kernels, run(): pl.pallas_call(kernel, out_shape=(out, out), in_specs=[smem, smem] + [pl....  85.3 us
    unnamed x4, local copies, waits for them, and re-layouts  2.15 us

profile of v9, /device:TPU:1, one launch (start us, length us, event | category | flops | bytes accessed | tf_op | source)
XLA Modules:
  0.0 88.1 jit_solution(7181835315473688391)
XLA Ops:
  0.6 85.3 %shard_map.68 = (f32[3,4096]{1,0:T(4,128)}, f32[3,4096]{1,0:T(4,128)}) custom-call(s32[2,2048]{1,0:T(2,128)} %bitcast.3, s32[256]{0:T(256)} %home_ref.1, s32[2,2048]{1,0:T(2,128)} %bitcast.4, s32[1,256]{1,0:T(1,128)} %bitcast.6, f32[3,4096]{1,0:T(4,128)} %pos_hbm.1, f32[3,4096]{1,0:T(4,128)} %str_hbm.1, f32[1,4096]{1,0:T(1,128)} %bitcast.5), custom_call_target="tpu_custom_call" | custom-call | tf_op jit(solution)/shard_map/pallas_call | solution.py:442
  86.0 0.0 copy-start
  86.0 1.5 %copy.9 = f32[3,4096]{1,0:T(4,128)} copy(f32[3,4096]{1,0:T(4,128)} %get-tuple-element.4) | data formatting | bytes 98304
  87.5 0.0 copy-done
  87.5 0.6 copy.10
Async XLA Ops:
  86.0 1.5 %copy-start = (f32[3,4096]{1,0:T(4,128)S(1)}, f32[3,4096]{1,0:T(4,128)}, u32[]{:S(2)}) copy-start(f32[3,4096]{1,0:T(4,128)} %get-tuple-element.5) | copy-start | bytes 147460
